TPU v7x, 32 devices: a whole 2x2x4 slice. The times are simulated.
32 devices in a mesh: groups: 2 (over y), pairs: 4 (over z), section: 2 (over core), sub: 2 (over x).
Axes of the slice: x: 2, y: 2, z: 4, core: 2. Of those that a mesh axis runs over, the one named last changes fastest.
Arguments:
- raw_record: bfloat16 [64, 49152], P(('groups', 'pairs', 'section'), 'sub'), parts along dimension 0, may hold values from -6 to 6
- fir_taps: float32 [64], replicated, may hold values from -0.75 to 0.75
- channel_ids: int32 [64], P('groups'), parts along dimension 0, may hold values from 0 to 31, each once
- offsets: int32 [8], P(('groups', 'sub')), parts along dimension 0, may hold values from 0 to 16324
- pair_table: int32 [32, 2], P('groups'), parts along dimension 0, may hold values from -1 to 3, as said below
Outputs:
- correlations: float32 [8, 32, 8, 2048], P(('section', 'sub'), ('groups', 'pairs')), parts along dimension 1
There are 2 independent parts, one for each index of `groups`. A program takes and returns all parts, laid end to end along the dimension named above; an argument that names none is the same for every part. Nothing has to cross between parts.
Inputs may be any that keep to these rules, and one draw needn't show every extreme that they name: `pair_table`: each row is a pair block (I, J) with I <= J, or (-1, -1) for an empty slot. Every pair block of the 4 x 4 triangle stands in exactly one slot; all live slots of one owner share the first block I; owners p and p + 2 together hold exactly 5 pair blocks; some owner fills all 4 slots.
All inputs are finite; a program needn't handle non-finite values.
Results may differ from a plain program's by a relative error of at most 0.0075.
Values may be sent and summed in bfloat16 or wider, within the bound.
No kernel may reach another device: no remote copies, remote signals or barrier semaphores. Data moves between devices by JAX's collectives and lax.ppermute only.
A program may use at most 128 MiB of HBM per device.

v0:
```python
import functools
import math

import jax
import jax.numpy as jnp
import ml_dtypes
import numpy as np
from jax import lax
from jax.experimental import pallas as pl
from jax.experimental.pallas import tpu as pltpu
from jax.sharding import PartitionSpec as P

NF = 2048
TAPS = 64
DEC = 4
BAND = 64
LANES = 128
HALF = LANES // 2
COARSE = NF // LANES

CHUNK_STEP = DEC * LANES // LANES
WINDOW_CHUNKS = CHUNK_STEP * (COARSE - 1) + 6
GRAIN = LANES // DEC


def two_terms(values):
    high = values.astype(ml_dtypes.bfloat16)
    low = (values - high.astype(np.float64)).astype(ml_dtypes.bfloat16)
    return high, low


def forward_constants(rows, windows):
    k1 = np.arange(COARSE)
    fine = np.arange(LANES)
    k2 = np.arange(HALF)
    angle_a = 2 * np.pi * np.outer(k1, np.arange(COARSE)) / COARSE
    count = rows * windows
    blocks = np.zeros((2, rows, windows, COARSE, windows, rows, COARSE))
    for r in range(rows):
        for w in range(windows):
            blocks[0, r, w, :, w, r, :] = np.cos(angle_a)
            blocks[1, r, w, :, w, r, :] = -np.sin(angle_a)
    high, low = two_terms(blocks.reshape(2 * count * COARSE, count * COARSE))
    step_a = np.concatenate([high, low], axis=1)
    angle_t = 2 * np.pi * np.outer(k1, fine) / NF
    twiddle = np.concatenate([np.cos(angle_t), -np.sin(angle_t)], axis=0).astype(np.float32)
    angle_b = 2 * np.pi * np.outer(fine, k2) / LANES
    cos_b, sin_b = np.cos(angle_b), np.sin(angle_b)
    table = np.concatenate(
        [np.concatenate([cos_b, -sin_b], axis=1), np.concatenate([sin_b, cos_b], axis=1)], axis=0
    )
    high, low = two_terms(table)
    step_b = np.concatenate([high, high, low], axis=0)
    band_of = np.tile(k2 * COARSE // BAND, 2)
    same_band = (band_of[:, None] == band_of[None, :]).astype(ml_dtypes.bfloat16)
    return step_a, twiddle, step_b, same_band


def inverse_constants(block_rows):
    k1 = np.arange(COARSE)
    k2 = np.arange(HALF)
    j1 = np.arange(LANES)
    angle_b = 2 * np.pi * np.outer(k2, j1) / LANES
    cos_b, sin_b = np.cos(angle_b), np.sin(angle_b)
    table = np.concatenate(
        [np.concatenate([cos_b, sin_b], axis=1), np.concatenate([-sin_b, cos_b], axis=1)], axis=0
    )
    step_b = np.concatenate(two_terms(table), axis=0)
    sign = np.where(k1 % 2 == 0, 1.0, -1.0)[:, None] / math.sqrt(NF)
    angle_t = 2 * np.pi * np.outer(k1, j1) / NF
    twiddle = np.concatenate([sign * np.cos(angle_t), sign * np.sin(angle_t)], axis=0)
    angle_a = 2 * np.pi * np.outer(np.arange(COARSE), k1) / COARSE
    blocks = np.zeros((COARSE, block_rows, 2, block_rows, COARSE))
    for b in range(block_rows):
        blocks[:, b, 0, b, :] = np.cos(angle_a)
        blocks[:, b, 1, b, :] = -np.sin(angle_a)
    high, low = two_terms(blocks.reshape(COARSE * block_rows, 2 * block_rows * COARSE))
    step_a = np.concatenate([high, high, low], axis=1)
    return step_b, twiddle.astype(np.float32), step_a


def split_terms(values):
    high = values.astype(jnp.bfloat16)
    low = (values - high.astype(jnp.float32)).astype(jnp.bfloat16)
    return high, low


def spectra_kernel(
    offsets_ref, taps_ref, raw_ref, step_a_ref, twiddle_ref, step_b_ref, band_ref, out_ref, chunks, padded
):
    rows = raw_ref.shape[0]
    windows = offsets_ref.shape[0]
    count = rows * windows
    chunk_total = raw_ref.shape[1] // LANES
    padded[...] = jnp.zeros_like(padded)
    padded[0:1, 0:TAPS] = taps_ref[...]
    plain = jnp.broadcast_to(padded[0:1, :], padded.shape)
    sublane = lax.broadcasted_iota(jnp.int32, padded.shape, 0)
    stair = plain
    for i in range(1, 8):
        stair = jnp.where(sublane == i, pltpu.roll(plain, DEC * i, 1), stair)
    stair = jnp.concatenate([stair, jnp.zeros((8, 2 * LANES), jnp.float32)], axis=1)
    empty = jnp.zeros((GRAIN, LANES), jnp.float32)
    parts = []
    for w in range(windows):
        start = offsets_ref[w]
        first = jnp.minimum(start // LANES, chunk_total - WINDOW_CHUNKS)
        shift = start - first * LANES
        slab = raw_ref[:, pl.ds(pl.multiple_of(first * LANES, LANES), WINDOW_CHUNKS * LANES)].astype(
            jnp.float32
        )
        for c in range(WINDOW_CHUNKS):
            chunks[w, rows * c : rows * (c + 1), :] = slab[:, c * LANES : (c + 1) * LANES]
        band = jnp.concatenate(
            [pltpu.roll(stair, shift + 8 * DEC * g, 1) for g in range(GRAIN // 8)], axis=0
        )
        left = []
        filt = []
        for m in range(6):
            pieces = [
                chunks[w, pl.ds(rows * m + r, COARSE, stride=rows * CHUNK_STEP), :] for r in range(rows)
            ]
            left.append(jnp.concatenate(pieces, axis=0).astype(jnp.bfloat16))
            column = [
                band[:, (m - g) * LANES : (m - g + 1) * LANES] if 0 <= m - g < 3 else empty
                for g in range(DEC)
            ]
            filt.append(jnp.concatenate(column, axis=0))
        left = jnp.concatenate(left, axis=1)
        filt = jnp.concatenate(split_terms(jnp.concatenate(filt, axis=1)), axis=0)
        both = lax.dot_general(
            left, filt, (((1,), (1,)), ((), ())), preferred_element_type=jnp.float32
        )
        parts.append((both[:, :LANES] + both[:, LANES:]).astype(jnp.bfloat16))
    decimated = jnp.concatenate(parts, axis=0)
    coarse = jnp.dot(
        step_a_ref[...], jnp.concatenate([decimated, decimated], axis=0), preferred_element_type=jnp.float32
    )
    size = count * COARSE
    real = coarse[:size].reshape(count, COARSE, LANES)
    imag = coarse[size:].reshape(count, COARSE, LANES)
    cos_t = twiddle_ref[:COARSE][None]
    sin_t = twiddle_ref[COARSE:][None]
    turned = jnp.concatenate(
        [
            (real * cos_t - imag * sin_t).reshape(size, LANES),
            (real * sin_t + imag * cos_t).reshape(size, LANES),
        ],
        axis=1,
    )
    high, low = split_terms(turned)
    spectrum = jnp.dot(
        jnp.concatenate([high, low, high], axis=1), step_b_ref[...], preferred_element_type=jnp.float32
    ).reshape(count, COARSE, LANES)
    power = jnp.sum(spectrum * spectrum, axis=1)
    high, low = split_terms(power)
    banded = jnp.dot(high, band_ref[...], preferred_element_type=jnp.float32) + jnp.dot(
        low, band_ref[...], preferred_element_type=jnp.float32
    )
    inverse_rms = lax.rsqrt(banded * (1.0 / BAND) + 1e-06)
    out_ref[...] = (spectrum * inverse_rms[:, None, :]).reshape(size, LANES).astype(jnp.bfloat16)


def correlate_kernel(
    plan, groups_of, ids_ref, table_ref, step_b_ref, twiddle_ref, step_a_ref, *refs
):
    piece_refs = refs[: len(plan)]
    out_ref, gathered, row_of = refs[len(plan) :]
    pairs, sections, subs = groups_of
    a_count, slots, block_rows = out_ref.shape[:3]
    rows_total, windows_total = gathered.shape[:2]
    channels = ids_ref.shape[0]
    rows = rows_total // (pairs * sections)
    windows = windows_total // subs
    tile = rows * windows * COARSE
    my_pair = lax.axis_index("pairs")
    my_section = lax.axis_index("section")
    my_sub = lax.axis_index("sub")

    for c in range(channels):
        row_of[ids_ref[c]] = c

    for ref, blocks in zip(piece_refs, plan):
        for q, (locate, offset) in enumerate(blocks):
            pair, section, sub = locate(my_pair, my_section, my_sub)
            base_row = (pair * sections + section) * rows
            base_window = sub * windows
            for r in range(rows):
                for w in range(windows):
                    at = offset + (r * windows + w) * COARSE
                    gathered[base_row + r, base_window + w] = ref[at : at + COARSE, :]

    lane = lax.broadcasted_iota(jnp.int32, (COARSE, LANES), 1)
    coarse_bin = lax.broadcasted_iota(jnp.int32, (COARSE, LANES), 0)
    in_left = lane < HALF
    is_zero_bin = (coarse_bin == 0) & (lane % HALF == 0)
    weight = jnp.where(is_zero_bin, 1.0, 2.0) * (1.0 / windows_total)
    cos_t = twiddle_ref[:COARSE][None]
    sin_t = twiddle_ref[COARSE:][None]
    size = block_rows * COARSE
    first_a = (my_section * subs + my_sub) * a_count

    def one_slot(s, carry):
        first_block = table_ref[my_pair * slots + s, 0]
        second_block = table_ref[my_pair * slots + s, 1]
        live = jnp.where(first_block >= 0, 1.0, 0.0)
        scale = weight * live
        first_block = jnp.maximum(first_block, 0)
        second_block = jnp.maximum(second_block, 0)
        ones, turns = [], []
        for a in range(a_count):
            row = row_of[first_block * block_rows + first_a + a]
            one = [gathered[row, w].astype(jnp.float32) for w in range(windows_total)]
            ones.append(one)
            turns.append([jnp.where(in_left, 1.0, -1.0) * pltpu.roll(v, HALF, 1) for v in one])
        crosses = [[] for _ in range(a_count)]
        for b in range(block_rows):
            row = row_of[second_block * block_rows + b]
            other = [gathered[row, w].astype(jnp.float32) for w in range(windows_total)]
            for a in range(a_count):
                even = ones[a][0] * other[0]
                odd = turns[a][0] * other[0]
                for w in range(1, windows_total):
                    even = even + ones[a][w] * other[w]
                    odd = odd + turns[a][w] * other[w]
                cross = jnp.where(in_left, even, odd) + pltpu.roll(jnp.where(in_left, odd, even), HALF, 1)
                crosses[a].append((cross * scale).astype(jnp.bfloat16))
        cross = jnp.concatenate([c for per_a in crosses for c in per_a], axis=0)
        fine = jnp.dot(
            jnp.concatenate([cross, cross], axis=1), step_b_ref[...], preferred_element_type=jnp.float32
        ).reshape(a_count * block_rows, COARSE, 2 * LANES)
        real, imag = fine[:, :, :LANES], fine[:, :, LANES:]
        turned_real = (real * cos_t - imag * sin_t).reshape(a_count, size, LANES)
        turned_imag = (real * sin_t + imag * cos_t).reshape(a_count, size, LANES)
        turned = jnp.concatenate(
            [
                jnp.concatenate([turned_real[a] for a in range(a_count)], axis=1),
                jnp.concatenate([turned_imag[a] for a in range(a_count)], axis=1),
            ],
            axis=0,
        )
        high, low = split_terms(turned)
        lags = jnp.dot(
            step_a_ref[...], jnp.concatenate([high, low, high], axis=0), preferred_element_type=jnp.float32
        )
        for a in range(a_count):
            for j2 in range(COARSE):
                out_ref[a, s, :, j2 * LANES : (j2 + 1) * LANES] = lags[
                    j2 * block_rows : (j2 + 1) * block_rows, a * LANES : (a + 1) * LANES
                ]
        return carry

    if slots <= 4:
        for s in range(slots):
            one_slot(s, 0)
    else:
        lax.fori_loop(0, slots, one_slot, 0)


def exchange(mine, sizes):
    pairs, sections, subs = sizes
    block = mine.shape[0]
    axes = ("pairs", "section", "sub")
    if (pairs, sections, subs) != (4, 2, 2):
        everything = lax.all_gather(mine, axes, axis=0, tiled=True)
        blocks = []
        for z in range(pairs):
            for s in range(sections):
                for x in range(subs):
                    blocks.append(
                        ((lambda p, q, u, z=z, s=s, x=x: (z, s, x)), ((z * sections + s) * subs + x) * block)
                    )
        return [everything], [blocks]

    def chips(value, *deltas):
        moves = []
        for z in range(pairs):
            for x in range(subs):
                for s in range(sections):
                    dz, dx = deltas[s % len(deltas)]
                    moves.append((((z * sections + s) * subs + x), ((z ^ dz) * sections + s) * subs + (x ^ dx)))
        return lax.ppermute(value, axes, moves)

    def cores(value):
        return lax.ppermute(value, "section", [(0, 1), (1, 0)])

    far = (3, 1)
    rounds = (((0, 1), (1, 0)), ((1, 1), (2, 0)), ((2, 1), (3, 0)))
    pieces = [mine]
    plan = [[((lambda p, q, u: (p, q, u)), 0)]]
    direct = chips(mine, far)
    other = cores(mine)
    pieces.append(other)
    plan.append([((lambda p, q, u: (p, 1 - q, u)), 0)])
    pieces.append(direct)
    plan.append([((lambda p, q, u: (p ^ far[0], q, u ^ far[1])), 0)])
    pieces.append(cores(direct))
    plan.append([((lambda p, q, u: (p ^ far[0], 1 - q, u ^ far[1])), 0)])
    both = jnp.concatenate([mine, other], axis=0)
    for d0, d1 in rounds:
        arrived = chips(both, d0, d1)

        def here(p, q, u, d0=d0, d1=d1):
            return (p ^ jnp.where(q == 0, d0[0], d1[0]), q, u ^ jnp.where(q == 0, d0[1], d1[1]))

        def here_flip(p, q, u, here=here):
            z, s, x = here(p, q, u)
            return z, 1 - s, x

        def there(p, q, u, here=here):
            return here(p, 1 - q, u)

        def there_flip(p, q, u, there=there):
            z, s, x = there(p, q, u)
            return z, 1 - s, x

        pieces.append(arrived)
        plan.append([(here, 0), (here_flip, block)])
        pieces.append(cores(arrived))
        plan.append([(there, 0), (there_flip, block)])
    return pieces, plan


def body(raw_record, fir_taps, channel_ids, offsets, pair_table):
    rows = raw_record.shape[0]
    windows = offsets.shape[0]
    sizes = tuple(lax.axis_size(name) for name in ("pairs", "section", "sub"))
    pairs, sections, subs = sizes
    block_rows = rows * sections
    slots = pair_table.shape[0] // pairs
    a_count = block_rows // (sections * subs)
    vmem = pl.BlockSpec(memory_space=pltpu.VMEM)
    smem = pl.BlockSpec(memory_space=pltpu.SMEM)

    consts = [jnp.asarray(c) for c in forward_constants(rows, windows)]
    whitened = pl.pallas_call(
        spectra_kernel,
        name="spectra",
        out_shape=jax.ShapeDtypeStruct((rows * windows * COARSE, LANES), jnp.bfloat16),
        in_specs=[smem] + [vmem] * 6,
        out_specs=vmem,
        scratch_shapes=[
            pltpu.VMEM((windows, rows * WINDOW_CHUNKS, LANES), jnp.float32),
            pltpu.VMEM((8, LANES), jnp.float32),
        ],
        compiler_params=pltpu.CompilerParams(vmem_limit_bytes=32 * 1024 * 1024),
    )(offsets, fir_taps.reshape(1, TAPS), raw_record, *consts)

    pieces, plan = exchange(whitened, sizes)

    consts = [jnp.asarray(c) for c in inverse_constants(block_rows)]
    return pl.pallas_call(
        functools.partial(correlate_kernel, plan, sizes),
        name="correlate",
        out_shape=jax.ShapeDtypeStruct((a_count, slots, block_rows, NF), jnp.float32),
        in_specs=[smem, smem] + [vmem] * (3 + len(pieces)),
        out_specs=vmem,
        scratch_shapes=[
            pltpu.VMEM((rows * pairs * sections, windows * subs, COARSE, LANES), jnp.bfloat16),
            pltpu.SMEM((channel_ids.shape[0],), jnp.int32),
        ],
        compiler_params=pltpu.CompilerParams(vmem_limit_bytes=32 * 1024 * 1024),
    )(channel_ids, pair_table, *consts, *pieces)


def solution(mesh):
    return jax.shard_map(
        body,
        mesh=mesh,
        in_specs=(
            P(("groups", "pairs", "section"), "sub"),
            P(),
            P("groups"),
            P(("groups", "sub")),
            P("groups", None),
        ),
        out_specs=P(("section", "sub"), ("groups", "pairs"), None, None),
        check_vma=False,
    )
```

profile of v0, /device:TPU:0, one launch (start us, length us, event | category | flops | bytes accessed | tf_op | source)
XLA Modules:
  0.0 26.5 jit_solution(16250701587138789011)
XLA Ops:
  0.0 0.0 copy-start.9
  0.0 0.0 copy-start.10
  0.0 0.7 %copy-done.9 = s32[2]{0:T(128)S(1)} copy-done((s32[2]{0:T(128)S(1)}, s32[2]{0:T(128)}, u32[]{:S(2)}) %copy-start.9) | copy-done | bytes 32
  0.7 0.0 copy-done.10
  0.7 0.0 copy-start.1
  0.7 0.9 %copy-done.1 = bf16[4,24576]{1,0:T(4,128)(2,1)S(1)} copy-done((bf16[4,24576]{1,0:T(4,128)(2,1)S(1)}, bf16[4,24576]{1,0:T(4,128)(2,1)}, u32[]{:S(2)}) %copy-start.1) | copy-done | bytes 196632
  1.6 0.0 copy-start.2
  1.6 0.9 %copy-done.2 = bf16[768,128]{1,0:T(8,128)(2,1)S(1)} copy-done((bf16[768,128]{1,0:T(8,128)(2,1)S(1)}, bf16[768,128]{1,0:T(8,128)(2,1)}, u32[]{:S(2)}) %copy-start.2) | copy-done | bytes 196632
  2.5 0.0 copy-start.4
  2.5 0.9 %copy-done.4 = bf16[256,256]{1,0:T(8,128)(2,1)S(1)} copy-done((bf16[256,256]{1,0:T(8,128)(2,1)S(1)}, bf16[256,256]{1,0:T(8,128)(2,1)}, u32[]{:S(2)}) %copy-start.4) | copy-done | bytes 131096
  3.4 0.0 copy-start.5
  3.4 0.8 %copy-done.5 = bf16[128,128]{1,0:T(8,128)(2,1)S(1)} copy-done((bf16[128,128]{1,0:T(8,128)(2,1)S(1)}, bf16[128,128]{1,0:T(8,128)(2,1)}, u32[]{:S(2)}) %copy-start.5) | copy-done | bytes 32792
  4.2 0.0 copy-start.7
  4.2 0.7 %copy-done.7 = f32[32,128]{1,0:T(8,128)S(1)} copy-done((f32[32,128]{1,0:T(8,128)S(1)}, f32[32,128]{1,0:T(8,128)}, u32[]{:S(2)}) %copy-start.7) | copy-done | bytes 16408
  4.9 0.0 copy-start.11
  4.9 0.0 copy-start
  4.9 0.0 copy-start.6
  4.9 1.6 %spectra.1.refs_0_ = bf16[128,128]{1,0:T(8,128)(2,1)S(1)} custom-call(s32[2]{0:T(128)S(1)} %copy-done.9, f32[1,64]{1,0:T(1,128)S(1)} %bitcast.1, bf16[4,24576]{1,0:T(4,128)(2,1)S(1)} %copy-done.1, bf16[256,256]{1,0:T(8,128)(2,1)S(1)} %copy-done.4, f32[32,128]{1,0:T(8,128)S(1)} %copy-done.7, bf16[768,128]{1,0:T(8,128)(2,1)S(1)} %copy-done.2, ...), custom_call_target="tpu_custom_call" | custom-call | tf_op jit(solution)/shard_map/spectra/pallas_call | solution.py:336
  6.5 0.0 copy-start.3
  6.5 0.5 %collective-permute-start = (bf16[128,128]{1,0:T(8,128)(2,1)S(1)}, bf16[128,128]{1,0:T(8,128)(2,1)S(1)}, u32[]{:S(2)}, u32[]{:S(2)}) collective-permute-start(bf16[128,128]{1,0:T(8,128)(2,1)S(1)} %spectra.1.refs_0_), channel_id=1, source_target_pairs={{0,2},{2,0},{1,3},{3,1},{4,6},{6,4},{5,7},{7,5},{8,10},{10,8},{9,1... | collective-permute-start | bytes 98312 | tf_op jit(solution)/shard_map/ppermute | solution.py:285
  7.0 0.9 %collective-permute-done.refs_1_ = bf16[128,128]{1,0:T(8,128)(2,1)S(1)} collective-permute-done((bf16[128,128]{1,0:T(8,128)(2,1)S(1)}, bf16[128,128]{1,0:T(8,128)(2,1)S(1)}, u32[]{:S(2)}, u32[]{:S(2)}) %collective-permute-start) | collective-permute-done | bytes 32800 | tf_op jit(solution)/shard_map/ppermute | solution.py:285
  7.9 0.0 copy-start.8
  7.9 4.9 %collective-permute-start.7 = (bf16[256,128]{1,0:T(8,128)(2,1)S(1)}, bf16[256,128]{1,0:T(8,128)(2,1)S(1)}, u32[]{:S(2)}, u32[]{:S(2)}) collective-permute-start(bf16[256,128]{1,0:T(8,128)(2,1)S(1)} %pad_maximum_fusion), channel_id=1, source_target_pairs={{0,9},{2,14},{1,8},{3,15},{4,13},{6,10},{5,12},{7,11},{8,1},{10,6}... | collective-permute-start | bytes 196616 | tf_op jit(solution)/shard_map/ppermute | solution.py:282
  12.8 1.5 %collective-permute-start.5 = (bf16[256,128]{1,0:T(8,128)(2,1)S(1)}, bf16[256,128]{1,0:T(8,128)(2,1)S(1)}, u32[]{:S(2)}, u32[]{:S(2)}) collective-permute-start(bf16[256,128]{1,0:T(8,128)(2,1)S(1)} %pad_maximum_fusion), channel_id=1, source_target_pairs={{0,5},{2,10},{1,4},{3,11},{4,1},{6,14},{5,0},{7,15},{8,13},{10,2},... | collective-permute-start | bytes 196616 | tf_op jit(solution)/shard_map/ppermute | solution.py:282
  14.4 1.5 %collective-permute-start.3 = (bf16[256,128]{1,0:T(8,128)(2,1)S(1)}, bf16[256,128]{1,0:T(8,128)(2,1)S(1)}, u32[]{:S(2)}, u32[]{:S(2)}) collective-permute-start(bf16[256,128]{1,0:T(8,128)(2,1)S(1)} %pad_maximum_fusion), channel_id=1, source_target_pairs={{0,1},{2,6},{1,0},{3,7},{4,5},{6,2},{5,4},{7,3},{8,9},{10,14},{9,8... | collective-permute-start | bytes 196616 | tf_op jit(solution)/shard_map/ppermute | solution.py:282
  15.9 0.0 collective-permute-start.1
  15.9 1.9 %collective-permute-done.7.refs_8_ = bf16[256,128]{1,0:T(8,128)(2,1)S(1)} collective-permute-done((bf16[256,128]{1,0:T(8,128)(2,1)S(1)}, bf16[256,128]{1,0:T(8,128)(2,1)S(1)}, u32[]{:S(2)}, u32[]{:S(2)}) %collective-permute-start.7) | collective-permute-done | bytes 65568 | tf_op jit(solution)/shard_map/ppermute | solution.py:282
  17.8 0.0 collective-permute-start.8
  17.8 1.2 %collective-permute-done.5.refs_6_ = bf16[256,128]{1,0:T(8,128)(2,1)S(1)} collective-permute-done((bf16[256,128]{1,0:T(8,128)(2,1)S(1)}, bf16[256,128]{1,0:T(8,128)(2,1)S(1)}, u32[]{:S(2)}, u32[]{:S(2)}) %collective-permute-start.5) | collective-permute-done | bytes 65568 | tf_op jit(solution)/shard_map/ppermute | solution.py:282
  19.0 0.0 collective-permute-start.6
  19.0 0.6 %collective-permute-done.3.refs_4_ = bf16[256,128]{1,0:T(8,128)(2,1)S(1)} collective-permute-done((bf16[256,128]{1,0:T(8,128)(2,1)S(1)}, bf16[256,128]{1,0:T(8,128)(2,1)S(1)}, u32[]{:S(2)}, u32[]{:S(2)}) %collective-permute-start.3) | collective-permute-done | bytes 65568 | tf_op jit(solution)/shard_map/ppermute | solution.py:282
  19.6 0.0 collective-permute-start.4
  19.6 2.8 %collective-permute-done.1.refs_2_ = bf16[128,128]{1,0:T(8,128)(2,1)S(1)} collective-permute-done((bf16[128,128]{1,0:T(8,128)(2,1)S(1)}, bf16[128,128]{1,0:T(8,128)(2,1)S(1)}, u32[]{:S(2)}, u32[]{:S(2)}) %collective-permute-start.1) | collective-permute-done | bytes 32800 | tf_op jit(solution)/shard_map/ppermute | solution.py:282
  22.5 0.0 collective-permute-start.2
  22.5 0.0 copy-done.11
  22.5 0.1 copy.13.table_ref
  22.6 1.1 %collective-permute-done.2.refs_3_ = bf16[128,128]{1,0:T(8,128)(2,1)S(1)} collective-permute-done((bf16[128,128]{1,0:T(8,128)(2,1)S(1)}, bf16[128,128]{1,0:T(8,128)(2,1)S(1)}, u32[]{:S(2)}, u32[]{:S(2)}) %collective-permute-start.2) | collective-permute-done | bytes 32800 | tf_op jit(solution)/shard_map/ppermute | solution.py:285
  23.7 0.0 collective-permute-done.8.refs_9_
  23.7 0.0 collective-permute-done.6.refs_7_
  23.7 0.0 collective-permute-done.4.refs_5_
  23.7 0.0 copy-done
  23.7 0.0 copy-done.6
  23.7 0.0 copy-done.3
  23.7 0.0 copy-done.8
  23.7 2.7 %correlate.1 = f32[2,4,8,2048]{3,2,1,0:T(8,128)} custom-call(s32[32]{0:T(128)S(1)} %copy-done.8, s32[16,2]{1,0:T(8,128)S(1)} %copy.13.table_ref, bf16[256,256]{1,0:T(8,128)(2,1)S(1)} %copy-done.3, f32[32,128]{1,0:T(8,128)S(1)} %copy-done.6, bf16[128,768]{1,0:T(8,128)(2,1)S(1)} %copy-done, bf16[128,128]{1,0:T(8,128)(2,1)S(1)} %spectra.1.refs_0_, ...), custom_call_target="tpu_custom_call" | custom-call | tf_op jit(solution)/shard_map/correlate/pallas_call | solution.py:352
  (1 shorter events, 0.0 us)
Async XLA Ops:
  0.0 0.7 %copy-start.9 = (s32[2]{0:T(128)S(1)}, s32[2]{0:T(128)}, u32[]{:S(2)}) copy-start(s32[2]{0:T(128)} %offsets_ref.1) | copy-start | bytes 28
  0.0 0.7 %copy-start.10 = (f32[64]{0:T(128)S(1)}, f32[64]{0:T(128)}, u32[]{:S(2)}) copy-start(f32[64]{0:T(128)} %param.13) | copy-start | bytes 772
  0.7 0.9 %copy-start.1 = (bf16[4,24576]{1,0:T(4,128)(2,1)S(1)}, bf16[4,24576]{1,0:T(4,128)(2,1)}, u32[]{:S(2)}) copy-start(bf16[4,24576]{1,0:T(4,128)(2,1)} %raw_ref.1) | copy-start | bytes 589828
  1.6 0.9 %copy-start.2 = (bf16[768,128]{1,0:T(8,128)(2,1)S(1)}, bf16[768,128]{1,0:T(8,128)(2,1)}, u32[]{:S(2)}) copy-start(bf16[768,128]{1,0:T(8,128)(2,1)} %constant.16.clone.step_b_ref) | copy-start | bytes 589828
  2.5 0.9 %copy-start.4 = (bf16[256,256]{1,0:T(8,128)(2,1)S(1)}, bf16[256,256]{1,0:T(8,128)(2,1)}, u32[]{:S(2)}) copy-start(bf16[256,256]{1,0:T(8,128)(2,1)} %constant.14.clone.step_a_ref) | copy-start | bytes 393220
  3.4 0.8 %copy-start.5 = (bf16[128,128]{1,0:T(8,128)(2,1)S(1)}, bf16[128,128]{1,0:T(8,128)(2,1)}, u32[]{:S(2)}) copy-start(bf16[128,128]{1,0:T(8,128)(2,1)} %constant.17.clone.band_ref) | copy-start | bytes 98308
  4.2 0.7 %copy-start.7 = (f32[32,128]{1,0:T(8,128)S(1)}, f32[32,128]{1,0:T(8,128)}, u32[]{:S(2)}) copy-start(f32[32,128]{1,0:T(8,128)} %constant.15.clone.twiddle_ref) | copy-start | bytes 49156
  4.9 17.6 %copy-start.11 = (s32[16,2]{0,1:T(2,128)S(1)}, s32[16,2]{0,1:T(2,128)}, u32[]{:S(2)}) copy-start(s32[16,2]{0,1:T(2,128)} %param.16) | copy-start | bytes 388
  4.9 18.8 %copy-start = (bf16[128,768]{1,0:T(8,128)(2,1)S(1)}, bf16[128,768]{1,0:T(8,128)(2,1)}, u32[]{:S(2)}) copy-start(bf16[128,768]{1,0:T(8,128)(2,1)} %constant.20.clone.step_a_ref) | copy-start | bytes 589828
  4.9 18.8 %copy-start.6 = (f32[32,128]{1,0:T(8,128)S(1)}, f32[32,128]{1,0:T(8,128)}, u32[]{:S(2)}) copy-start(f32[32,128]{1,0:T(8,128)} %constant.19.clone.twiddle_ref) | copy-start | bytes 49156
  6.5 17.2 %copy-start.3 = (bf16[256,256]{1,0:T(8,128)(2,1)S(1)}, bf16[256,256]{1,0:T(8,128)(2,1)}, u32[]{:S(2)}) copy-start(bf16[256,256]{1,0:T(8,128)(2,1)} %constant.18.clone.step_b_ref) | copy-start | bytes 393220
  6.5 1.4 %collective-permute-start = (bf16[128,128]{1,0:T(8,128)(2,1)S(1)}, bf16[128,128]{1,0:T(8,128)(2,1)S(1)}, u32[]{:S(2)}, u32[]{:S(2)}) collective-permute-start(bf16[128,128]{1,0:T(8,128)(2,1)S(1)} %spectra.1.refs_0_), channel_id=1, source_target_pairs={{0,2},{2,0},{1,3},{3,1},{4,6},{6,4},{5,7},{7,5},{8,10},{10,8},{9,1... | collective-permute-start | bytes 98312 | tf_op jit(solution)/shard_map/ppermute | solution.py:285
  7.9 15.8 %copy-start.8 = (s32[32]{0:T(128)S(1)}, s32[32]{0:T(128)}, u32[]{:S(2)}) copy-start(s32[32]{0:T(128)} %ids_ref.1) | copy-start | bytes 388
  7.9 9.8 %collective-permute-start.7 = (bf16[256,128]{1,0:T(8,128)(2,1)S(1)}, bf16[256,128]{1,0:T(8,128)(2,1)S(1)}, u32[]{:S(2)}, u32[]{:S(2)}) collective-permute-start(bf16[256,128]{1,0:T(8,128)(2,1)S(1)} %pad_maximum_fusion), channel_id=1, source_target_pairs={{0,9},{2,14},{1,8},{3,15},{4,13},{6,10},{5,12},{7,11},{8,1},{10,6}... | collective-permute-start | bytes 196616 | tf_op jit(solution)/shard_map/ppermute | solution.py:282
  12.8 6.2 %collective-permute-start.5 = (bf16[256,128]{1,0:T(8,128)(2,1)S(1)}, bf16[256,128]{1,0:T(8,128)(2,1)S(1)}, u32[]{:S(2)}, u32[]{:S(2)}) collective-permute-start(bf16[256,128]{1,0:T(8,128)(2,1)S(1)} %pad_maximum_fusion), channel_id=1, source_target_pairs={{0,5},{2,10},{1,4},{3,11},{4,1},{6,14},{5,0},{7,15},{8,13},{10,2},... | collective-permute-start | bytes 196616 | tf_op jit(solution)/shard_map/ppermute | solution.py:282
  14.4 5.3 %collective-permute-start.3 = (bf16[256,128]{1,0:T(8,128)(2,1)S(1)}, bf16[256,128]{1,0:T(8,128)(2,1)S(1)}, u32[]{:S(2)}, u32[]{:S(2)}) collective-permute-start(bf16[256,128]{1,0:T(8,128)(2,1)S(1)} %pad_maximum_fusion), channel_id=1, source_target_pairs={{0,1},{2,6},{1,0},{3,7},{4,5},{6,2},{5,4},{7,3},{8,9},{10,14},{9,8... | collective-permute-start | bytes 196616 | tf_op jit(solution)/shard_map/ppermute | solution.py:282
  15.9 6.6 %collective-permute-start.1 = (bf16[128,128]{1,0:T(8,128)(2,1)S(1)}, bf16[128,128]{1,0:T(8,128)(2,1)S(1)}, u32[]{:S(2)}, u32[]{:S(2)}) collective-permute-start(bf16[128,128]{1,0:T(8,128)(2,1)S(1)} %spectra.1.refs_0_), channel_id=1, source_target_pairs={{0,13},{2,15},{1,12},{3,14},{4,9},{6,11},{5,8},{7,10},{8,5},{10,7}... | collective-permute-start | bytes 98312 | tf_op jit(solution)/shard_map/ppermute | solution.py:282
  17.8 5.9 %collective-permute-start.8 = (bf16[256,128]{1,0:T(8,128)(2,1)S(1)}, bf16[256,128]{1,0:T(8,128)(2,1)S(1)}, u32[]{:S(2)}, u32[]{:S(2)}) collective-permute-start(bf16[256,128]{1,0:T(8,128)(2,1)S(1)} %collective-permute-done.7.refs_8_), channel_id=1, source_target_pairs={{0,2},{2,0},{1,3},{3,1},{4,6},{6,4},{5,7},{7,5},{8,10},{10,8},{9,1... | collective-permute-start | bytes 196616 | tf_op jit(solution)/shard_map/ppermute | solution.py:285
  19.0 4.7 %collective-permute-start.6 = (bf16[256,128]{1,0:T(8,128)(2,1)S(1)}, bf16[256,128]{1,0:T(8,128)(2,1)S(1)}, u32[]{:S(2)}, u32[]{:S(2)}) collective-permute-start(bf16[256,128]{1,0:T(8,128)(2,1)S(1)} %collective-permute-done.5.refs_6_), channel_id=1, source_target_pairs={{0,2},{2,0},{1,3},{3,1},{4,6},{6,4},{5,7},{7,5},{8,10},{10,8},{9,1... | collective-permute-start | bytes 196616 | tf_op jit(solution)/shard_map/ppermute | solution.py:285
  19.6 4.1 %collective-permute-start.4 = (bf16[256,128]{1,0:T(8,128)(2,1)S(1)}, bf16[256,128]{1,0:T(8,128)(2,1)S(1)}, u32[]{:S(2)}, u32[]{:S(2)}) collective-permute-start(bf16[256,128]{1,0:T(8,128)(2,1)S(1)} %collective-permute-done.3.refs_4_), channel_id=1, source_target_pairs={{0,2},{2,0},{1,3},{3,1},{4,6},{6,4},{5,7},{7,5},{8,10},{10,8},{9,1... | collective-permute-start | bytes 196616 | tf_op jit(solution)/shard_map/ppermute | solution.py:285
  22.5 1.2 %collective-permute-start.2 = (bf16[128,128]{1,0:T(8,128)(2,1)S(1)}, bf16[128,128]{1,0:T(8,128)(2,1)S(1)}, u32[]{:S(2)}, u32[]{:S(2)}) collective-permute-start(bf16[128,128]{1,0:T(8,128)(2,1)S(1)} %collective-permute-done.1.refs_2_), channel_id=1, source_target_pairs={{0,2},{2,0},{1,3},{3,1},{4,6},{6,4},{5,7},{7,5},{8,10},{10,8},{9,1... | collective-permute-start | bytes 98312 | tf_op jit(solution)/shard_map/ppermute | solution.py:285
where the time goes:
time: 26.8 us; the launch traced here: 26.5 us
  waiting for transfers between devices  8.58 us (32%)
  starting transfers between devices  8.5 us (32%)
  local copies, waits for them, and re-layouts  5 us (19%)
  Pallas kernels  4.33 us (16%)
    ppermute x4, starting transfers between devices, chips(): return lax.ppermute(value, axes, moves)  7.97 us
    ppermute x4, waiting for transfers between devices, chips(): return lax.ppermute(value, axes, moves)  6.6 us
    unnamed x25, local copies, waits for them, and re-layouts  5 us
    pallas_call x1, Pallas kernels, body(): pl.pallas_call(functools.partial(correlate_kernel, plan, sizes), name='co...  2.75 us
    ppermute x5, waiting for transfers between devices, cores(): return lax.ppermute(value, 'section', [(0, 1), (1, 0)])  1.99 us
    pallas_call x1, Pallas kernels, body(): pl.pallas_call(spectra_kernel, name='spectra', out_shape=jax.ShapeDtypeSt...  1.59 us
  transfers between devices with their start and end apart: 9, of which 6 were waited for; matrix products, arithmetic and copies ran while one was open for 0% of the time, Pallas kernels for 0%

commit v1 on v0

--- a/solution.py
+++ b/solution.py
@@ -86,13 +86,39 @@
 
 
 def spectra_kernel(
-    offsets_ref, taps_ref, raw_ref, step_a_ref, twiddle_ref, step_b_ref, band_ref, out_ref, chunks, padded
+    offsets_hbm,
+    taps_hbm,
+    raw_hbm,
+    step_a_hbm,
+    twiddle_hbm,
+    step_b_hbm,
+    band_hbm,
+    out_ref,
+    offsets_ref,
+    taps_ref,
+    raw_ref,
+    step_a_ref,
+    twiddle_ref,
+    step_b_ref,
+    band_ref,
+    chunks,
+    padded,
+    arrived,
 ):
+    sources = (offsets_hbm, taps_hbm, raw_hbm, step_a_hbm, twiddle_hbm, step_b_hbm, band_hbm)
+    places = (offsets_ref, taps_ref, raw_ref, step_a_ref, twiddle_ref, step_b_ref, band_ref)
+    copies = [
+        pltpu.make_async_copy(source, place, arrived.at[q])
+        for q, (source, place) in enumerate(zip(sources, places))
+    ]
+    for copy in copies:
+        copy.start()
     rows = raw_ref.shape[0]
     windows = offsets_ref.shape[0]
     count = rows * windows
     chunk_total = raw_ref.shape[1] // LANES
     padded[...] = jnp.zeros_like(padded)
+    copies[1].wait()
     padded[0:1, 0:TAPS] = taps_ref[...]
     plain = jnp.broadcast_to(padded[0:1, :], padded.shape)
     sublane = lax.broadcasted_iota(jnp.int32, padded.shape, 0)
@@ -102,6 +128,8 @@
     stair = jnp.concatenate([stair, jnp.zeros((8, 2 * LANES), jnp.float32)], axis=1)
     empty = jnp.zeros((GRAIN, LANES), jnp.float32)
     parts = []
+    copies[0].wait()
+    copies[2].wait()
     for w in range(windows):
         start = offsets_ref[w]
         first = jnp.minimum(start // LANES, chunk_total - WINDOW_CHUNKS)
@@ -133,12 +161,14 @@
         )
         parts.append((both[:, :LANES] + both[:, LANES:]).astype(jnp.bfloat16))
     decimated = jnp.concatenate(parts, axis=0)
+    copies[3].wait()
     coarse = jnp.dot(
         step_a_ref[...], jnp.concatenate([decimated, decimated], axis=0), preferred_element_type=jnp.float32
     )
     size = count * COARSE
     real = coarse[:size].reshape(count, COARSE, LANES)
     imag = coarse[size:].reshape(count, COARSE, LANES)
+    copies[4].wait()
     cos_t = twiddle_ref[:COARSE][None]
     sin_t = twiddle_ref[COARSE:][None]
     turned = jnp.concatenate(
@@ -149,11 +179,13 @@
         axis=1,
     )
     high, low = split_terms(turned)
+    copies[5].wait()
     spectrum = jnp.dot(
         jnp.concatenate([high, low, high], axis=1), step_b_ref[...], preferred_element_type=jnp.float32
     ).reshape(count, COARSE, LANES)
     power = jnp.sum(spectrum * spectrum, axis=1)
     high, low = split_terms(power)
+    copies[6].wait()
     banded = jnp.dot(high, band_ref[...], preferred_element_type=jnp.float32) + jnp.dot(
         low, band_ref[...], preferred_element_type=jnp.float32
     )
@@ -332,19 +364,24 @@
     vmem = pl.BlockSpec(memory_space=pltpu.VMEM)
     smem = pl.BlockSpec(memory_space=pltpu.SMEM)
 
-    consts = [jnp.asarray(c) for c in forward_constants(rows, windows)]
+    operands = [offsets, fir_taps.reshape(1, TAPS), raw_record]
+    operands += [jnp.asarray(c) for c in forward_constants(rows, windows)]
+    operands = [pltpu.with_memory_space_constraint(operand, pltpu.HBM) for operand in operands]
     whitened = pl.pallas_call(
         spectra_kernel,
         name="spectra",
-        out_shape=jax.ShapeDtypeStruct((rows * windows * COARSE, LANES), jnp.bfloat16),
-        in_specs=[smem] + [vmem] * 6,
+        out_shape=pltpu.VMEM((rows * windows * COARSE, LANES), jnp.bfloat16),
+        in_specs=[pl.BlockSpec(memory_space=pltpu.HBM)] * len(operands),
         out_specs=vmem,
-        scratch_shapes=[
+        scratch_shapes=[pltpu.SMEM(offsets.shape, offsets.dtype)]
+        + [pltpu.VMEM(operand.shape, operand.dtype) for operand in operands[1:]]
+        + [
             pltpu.VMEM((windows, rows * WINDOW_CHUNKS, LANES), jnp.float32),
             pltpu.VMEM((8, LANES), jnp.float32),
+            pltpu.SemaphoreType.DMA((len(operands),)),
         ],
         compiler_params=pltpu.CompilerParams(vmem_limit_bytes=32 * 1024 * 1024),
-    )(offsets, fir_taps.reshape(1, TAPS), raw_record, *consts)
+    )(*operands)
 
     pieces, plan = exchange(whitened, sizes)
 

time: 26.8 us -> 22.3 us (0.83)
  local copies, waits for them, and re-layouts: 5 us -> 0.1 us
  Pallas kernels: 4.33 us -> 4.87 us
    unnamed x25 -> x11, local copies, waits for them, and re-layouts: 5 us -> 0.1 us
    pallas_call x1, Pallas kernels: 1.59 us -> 2.13 us  [body(): pl.pallas_call(spectra_kernel, name='spectra', out_shape=pltpu.VMEM((rows...]
where the time goes in v1:
time: 22.3 us; the launch traced here: 22.1 us
  waiting for transfers between devices  8.58 us (38%)
  starting transfers between devices  8.51 us (38%)
  Pallas kernels  4.87 us (22%)
    ppermute x4, starting transfers between devices, chips(): return lax.ppermute(value, axes, moves)  7.97 us
    ppermute x4, waiting for transfers between devices, chips(): return lax.ppermute(value, axes, moves)  6.6 us
    pallas_call x1, Pallas kernels, body(): pl.pallas_call(functools.partial(correlate_kernel, plan, sizes), name='co...  2.75 us
    pallas_call x1, Pallas kernels, body(): pl.pallas_call(spectra_kernel, name='spectra', out_shape=pltpu.VMEM((rows...  2.13 us
    ppermute x5, waiting for transfers between devices, cores(): return lax.ppermute(value, 'section', [(0, 1), (1, 0)])  1.99 us
    ppermute x5, starting transfers between devices, cores(): return lax.ppermute(value, 'section', [(0, 1), (1, 0)])  0.54 us
  transfers between devices with their start and end apart: 9, of which 6 were waited for; matrix products, arithmetic and copies ran while one was open for 0% of the time, Pallas kernels for 0%

profile of v1, /device:TPU:0, one launch (start us, length us, event | category | flops | bytes accessed | tf_op | source)
XLA Modules:
  0.0 22.1 jit_solution(12643113140151887815)
XLA Ops:
  0.0 0.0 copy-start.4
  0.0 0.0 copy-start
  0.0 0.0 copy-start.2
  0.0 2.1 %spectra.1.refs_0_ = bf16[128,128]{1,0:T(8,128)(2,1)S(1)} custom-call(s32[2]{0:T(128)} %offsets_hbm.1, f32[1,64]{1,0:T(1,128)} %bitcast.1, bf16[4,24576]{1,0:T(4,128)(2,1)} %raw_hbm.1, bf16[256,256]{1,0:T(8,128)(2,1)} %constant.14.clone.step_a_hbm, f32[32,128]{1,0:T(8,128)} %constant.15.clone.twiddle_hbm, bf16[768,128]{1,0:T(8,128)(2,1)} %constant.16.clone.step_b_hbm, ...), custom_call_target="tpu_custom_call" | custom-call | tf_op jit(solution)/shard_map/spectra/pallas_call | solution.py:370
  2.1 0.0 copy-start.1
  2.2 0.5 %collective-permute-start = (bf16[128,128]{1,0:T(8,128)(2,1)S(1)}, bf16[128,128]{1,0:T(8,128)(2,1)S(1)}, u32[]{:S(2)}, u32[]{:S(2)}) collective-permute-start(bf16[128,128]{1,0:T(8,128)(2,1)S(1)} %spectra.1.refs_0_), channel_id=1, source_target_pairs={{0,2},{2,0},{1,3},{3,1},{4,6},{6,4},{5,7},{7,5},{8,10},{10,8},{9,1... | collective-permute-start | bytes 98312 | tf_op jit(solution)/shard_map/ppermute | solution.py:317
  2.7 0.9 %collective-permute-done.refs_1_ = bf16[128,128]{1,0:T(8,128)(2,1)S(1)} collective-permute-done((bf16[128,128]{1,0:T(8,128)(2,1)S(1)}, bf16[128,128]{1,0:T(8,128)(2,1)S(1)}, u32[]{:S(2)}, u32[]{:S(2)}) %collective-permute-start) | collective-permute-done | bytes 32800 | tf_op jit(solution)/shard_map/ppermute | solution.py:317
  3.5 0.0 copy-start.3
  3.5 4.9 %collective-permute-start.7 = (bf16[256,128]{1,0:T(8,128)(2,1)S(1)}, bf16[256,128]{1,0:T(8,128)(2,1)S(1)}, u32[]{:S(2)}, u32[]{:S(2)}) collective-permute-start(bf16[256,128]{1,0:T(8,128)(2,1)S(1)} %pad_maximum_fusion), channel_id=1, source_target_pairs={{0,9},{2,14},{1,8},{3,15},{4,13},{6,10},{5,12},{7,11},{8,1},{10,6}... | collective-permute-start | bytes 196616 | tf_op jit(solution)/shard_map/ppermute | solution.py:314
  8.5 1.5 %collective-permute-start.5 = (bf16[256,128]{1,0:T(8,128)(2,1)S(1)}, bf16[256,128]{1,0:T(8,128)(2,1)S(1)}, u32[]{:S(2)}, u32[]{:S(2)}) collective-permute-start(bf16[256,128]{1,0:T(8,128)(2,1)S(1)} %pad_maximum_fusion), channel_id=1, source_target_pairs={{0,5},{2,10},{1,4},{3,11},{4,1},{6,14},{5,0},{7,15},{8,13},{10,2},... | collective-permute-start | bytes 196616 | tf_op jit(solution)/shard_map/ppermute | solution.py:314
  10.0 1.5 %collective-permute-start.3 = (bf16[256,128]{1,0:T(8,128)(2,1)S(1)}, bf16[256,128]{1,0:T(8,128)(2,1)S(1)}, u32[]{:S(2)}, u32[]{:S(2)}) collective-permute-start(bf16[256,128]{1,0:T(8,128)(2,1)S(1)} %pad_maximum_fusion), channel_id=1, source_target_pairs={{0,1},{2,6},{1,0},{3,7},{4,5},{6,2},{5,4},{7,3},{8,9},{10,14},{9,8... | collective-permute-start | bytes 196616 | tf_op jit(solution)/shard_map/ppermute | solution.py:314
  11.5 0.0 collective-permute-start.1
  11.5 1.9 %collective-permute-done.7.refs_8_ = bf16[256,128]{1,0:T(8,128)(2,1)S(1)} collective-permute-done((bf16[256,128]{1,0:T(8,128)(2,1)S(1)}, bf16[256,128]{1,0:T(8,128)(2,1)S(1)}, u32[]{:S(2)}, u32[]{:S(2)}) %collective-permute-start.7) | collective-permute-done | bytes 65568 | tf_op jit(solution)/shard_map/ppermute | solution.py:314
  13.4 0.0 collective-permute-start.8
  13.4 1.2 %collective-permute-done.5.refs_6_ = bf16[256,128]{1,0:T(8,128)(2,1)S(1)} collective-permute-done((bf16[256,128]{1,0:T(8,128)(2,1)S(1)}, bf16[256,128]{1,0:T(8,128)(2,1)S(1)}, u32[]{:S(2)}, u32[]{:S(2)}) %collective-permute-start.5) | collective-permute-done | bytes 65568 | tf_op jit(solution)/shard_map/ppermute | solution.py:314
  14.6 0.0 collective-permute-start.6
  14.6 0.6 %collective-permute-done.3.refs_4_ = bf16[256,128]{1,0:T(8,128)(2,1)S(1)} collective-permute-done((bf16[256,128]{1,0:T(8,128)(2,1)S(1)}, bf16[256,128]{1,0:T(8,128)(2,1)S(1)}, u32[]{:S(2)}, u32[]{:S(2)}) %collective-permute-start.3) | collective-permute-done | bytes 65568 | tf_op jit(solution)/shard_map/ppermute | solution.py:314
  15.3 0.0 collective-permute-start.4
  15.3 2.8 %collective-permute-done.1.refs_2_ = bf16[128,128]{1,0:T(8,128)(2,1)S(1)} collective-permute-done((bf16[128,128]{1,0:T(8,128)(2,1)S(1)}, bf16[128,128]{1,0:T(8,128)(2,1)S(1)}, u32[]{:S(2)}, u32[]{:S(2)}) %collective-permute-start.1) | collective-permute-done | bytes 32800 | tf_op jit(solution)/shard_map/ppermute | solution.py:314
  18.1 0.0 collective-permute-start.2
  18.1 0.0 copy-done.4
  18.1 0.1 copy.13.table_ref
  18.2 1.1 %collective-permute-done.2.refs_3_ = bf16[128,128]{1,0:T(8,128)(2,1)S(1)} collective-permute-done((bf16[128,128]{1,0:T(8,128)(2,1)S(1)}, bf16[128,128]{1,0:T(8,128)(2,1)S(1)}, u32[]{:S(2)}, u32[]{:S(2)}) %collective-permute-start.2) | collective-permute-done | bytes 32800 | tf_op jit(solution)/shard_map/ppermute | solution.py:317
  19.3 0.0 collective-permute-done.8.refs_9_
  19.3 0.0 collective-permute-done.6.refs_7_
  19.3 0.0 collective-permute-done.4.refs_5_
  19.4 0.0 copy-done
  19.4 0.0 copy-done.2
  19.4 0.0 copy-done.1
  19.4 0.0 copy-done.3
  19.4 2.7 %correlate.1 = f32[2,4,8,2048]{3,2,1,0:T(8,128)} custom-call(s32[32]{0:T(128)S(1)} %copy-done.3, s32[16,2]{1,0:T(8,128)S(1)} %copy.13.table_ref, bf16[256,256]{1,0:T(8,128)(2,1)S(1)} %copy-done.1, f32[32,128]{1,0:T(8,128)S(1)} %copy-done.2, bf16[128,768]{1,0:T(8,128)(2,1)S(1)} %copy-done, bf16[128,128]{1,0:T(8,128)(2,1)S(1)} %spectra.1.refs_0_, ...), custom_call_target="tpu_custom_call" | custom-call | tf_op jit(solution)/shard_map/correlate/pallas_call | solution.py:389
  (1 shorter events, 0.0 us)
Async XLA Ops:
  0.0 18.1 %copy-start.4 = (s32[16,2]{0,1:T(2,128)S(1)}, s32[16,2]{0,1:T(2,128)}, u32[]{:S(2)}) copy-start(s32[16,2]{0,1:T(2,128)} %param.16) | copy-start | bytes 388
  0.0 19.3 %copy-start = (bf16[128,768]{1,0:T(8,128)(2,1)S(1)}, bf16[128,768]{1,0:T(8,128)(2,1)}, u32[]{:S(2)}) copy-start(bf16[128,768]{1,0:T(8,128)(2,1)} %constant.20.clone.step_a_ref) | copy-start | bytes 589828
  0.0 19.4 %copy-start.2 = (f32[32,128]{1,0:T(8,128)S(1)}, f32[32,128]{1,0:T(8,128)}, u32[]{:S(2)}) copy-start(f32[32,128]{1,0:T(8,128)} %constant.19.clone.twiddle_ref) | copy-start | bytes 49156
  2.1 17.2 %copy-start.1 = (bf16[256,256]{1,0:T(8,128)(2,1)S(1)}, bf16[256,256]{1,0:T(8,128)(2,1)}, u32[]{:S(2)}) copy-start(bf16[256,256]{1,0:T(8,128)(2,1)} %constant.18.clone.step_b_ref) | copy-start | bytes 393220
  2.2 1.4 %collective-permute-start = (bf16[128,128]{1,0:T(8,128)(2,1)S(1)}, bf16[128,128]{1,0:T(8,128)(2,1)S(1)}, u32[]{:S(2)}, u32[]{:S(2)}) collective-permute-start(bf16[128,128]{1,0:T(8,128)(2,1)S(1)} %spectra.1.refs_0_), channel_id=1, source_target_pairs={{0,2},{2,0},{1,3},{3,1},{4,6},{6,4},{5,7},{7,5},{8,10},{10,8},{9,1... | collective-permute-start | bytes 98312 | tf_op jit(solution)/shard_map/ppermute | solution.py:317
  3.5 15.8 %copy-start.3 = (s32[32]{0:T(128)S(1)}, s32[32]{0:T(128)}, u32[]{:S(2)}) copy-start(s32[32]{0:T(128)} %ids_ref.1) | copy-start | bytes 388
  3.5 9.8 %collective-permute-start.7 = (bf16[256,128]{1,0:T(8,128)(2,1)S(1)}, bf16[256,128]{1,0:T(8,128)(2,1)S(1)}, u32[]{:S(2)}, u32[]{:S(2)}) collective-permute-start(bf16[256,128]{1,0:T(8,128)(2,1)S(1)} %pad_maximum_fusion), channel_id=1, source_target_pairs={{0,9},{2,14},{1,8},{3,15},{4,13},{6,10},{5,12},{7,11},{8,1},{10,6}... | collective-permute-start | bytes 196616 | tf_op jit(solution)/shard_map/ppermute | solution.py:314
  8.5 6.2 %collective-permute-start.5 = (bf16[256,128]{1,0:T(8,128)(2,1)S(1)}, bf16[256,128]{1,0:T(8,128)(2,1)S(1)}, u32[]{:S(2)}, u32[]{:S(2)}) collective-permute-start(bf16[256,128]{1,0:T(8,128)(2,1)S(1)} %pad_maximum_fusion), channel_id=1, source_target_pairs={{0,5},{2,10},{1,4},{3,11},{4,1},{6,14},{5,0},{7,15},{8,13},{10,2},... | collective-permute-start | bytes 196616 | tf_op jit(solution)/shard_map/ppermute | solution.py:314
  10.0 5.3 %collective-permute-start.3 = (bf16[256,128]{1,0:T(8,128)(2,1)S(1)}, bf16[256,128]{1,0:T(8,128)(2,1)S(1)}, u32[]{:S(2)}, u32[]{:S(2)}) collective-permute-start(bf16[256,128]{1,0:T(8,128)(2,1)S(1)} %pad_maximum_fusion), channel_id=1, source_target_pairs={{0,1},{2,6},{1,0},{3,7},{4,5},{6,2},{5,4},{7,3},{8,9},{10,14},{9,8... | collective-permute-start | bytes 196616 | tf_op jit(solution)/shard_map/ppermute | solution.py:314
  11.5 6.6 %collective-permute-start.1 = (bf16[128,128]{1,0:T(8,128)(2,1)S(1)}, bf16[128,128]{1,0:T(8,128)(2,1)S(1)}, u32[]{:S(2)}, u32[]{:S(2)}) collective-permute-start(bf16[128,128]{1,0:T(8,128)(2,1)S(1)} %spectra.1.refs_0_), channel_id=1, source_target_pairs={{0,13},{2,15},{1,12},{3,14},{4,9},{6,11},{5,8},{7,10},{8,5},{10,7}... | collective-permute-start | bytes 98312 | tf_op jit(solution)/shard_map/ppermute | solution.py:314
  13.4 5.9 %collective-permute-start.8 = (bf16[256,128]{1,0:T(8,128)(2,1)S(1)}, bf16[256,128]{1,0:T(8,128)(2,1)S(1)}, u32[]{:S(2)}, u32[]{:S(2)}) collective-permute-start(bf16[256,128]{1,0:T(8,128)(2,1)S(1)} %collective-permute-done.7.refs_8_), channel_id=1, source_target_pairs={{0,2},{2,0},{1,3},{3,1},{4,6},{6,4},{5,7},{7,5},{8,10},{10,8},{9,1... | collective-permute-start | bytes 196616 | tf_op jit(solution)/shard_map/ppermute | solution.py:317
  14.6 4.7 %collective-permute-start.6 = (bf16[256,128]{1,0:T(8,128)(2,1)S(1)}, bf16[256,128]{1,0:T(8,128)(2,1)S(1)}, u32[]{:S(2)}, u32[]{:S(2)}) collective-permute-start(bf16[256,128]{1,0:T(8,128)(2,1)S(1)} %collective-permute-done.5.refs_6_), channel_id=1, source_target_pairs={{0,2},{2,0},{1,3},{3,1},{4,6},{6,4},{5,7},{7,5},{8,10},{10,8},{9,1... | collective-permute-start | bytes 196616 | tf_op jit(solution)/shard_map/ppermute | solution.py:317
  15.3 4.1 %collective-permute-start.4 = (bf16[256,128]{1,0:T(8,128)(2,1)S(1)}, bf16[256,128]{1,0:T(8,128)(2,1)S(1)}, u32[]{:S(2)}, u32[]{:S(2)}) collective-permute-start(bf16[256,128]{1,0:T(8,128)(2,1)S(1)} %collective-permute-done.3.refs_4_), channel_id=1, source_target_pairs={{0,2},{2,0},{1,3},{3,1},{4,6},{6,4},{5,7},{7,5},{8,10},{10,8},{9,1... | collective-permute-start | bytes 196616 | tf_op jit(solution)/shard_map/ppermute | solution.py:317
  18.1 1.2 %collective-permute-start.2 = (bf16[128,128]{1,0:T(8,128)(2,1)S(1)}, bf16[128,128]{1,0:T(8,128)(2,1)S(1)}, u32[]{:S(2)}, u32[]{:S(2)}) collective-permute-start(bf16[128,128]{1,0:T(8,128)(2,1)S(1)} %collective-permute-done.1.refs_2_), channel_id=1, source_target_pairs={{0,2},{2,0},{1,3},{3,1},{4,6},{6,4},{5,7},{7,5},{8,10},{10,8},{9,1... | collective-permute-start | bytes 98312 | tf_op jit(solution)/shard_map/ppermute | solution.py:317

commit v2 on v1

--- a/solution.py
+++ b/solution.py
@@ -20,6 +20,8 @@
 
 CHUNK_STEP = DEC * LANES // LANES
 WINDOW_CHUNKS = CHUNK_STEP * (COARSE - 1) + 6
+STEPS = (((1, 0), (1, 0), 'own'), ((2, 0), (2, 1), 'both'), ((3, 0), (3, 1), 'both'), ((0, 1), (1, 1), 'both'))
+ORDER = (3, 2, 1, 0)
 GRAIN = LANES // DEC
 
 
@@ -316,21 +318,27 @@
     def cores(value):
         return lax.ppermute(value, "section", [(0, 1), (1, 0)])
 
-    far = (3, 1)
-    rounds = (((0, 1), (1, 0)), ((1, 1), (2, 0)), ((2, 1), (3, 0)))
     pieces = [mine]
     plan = [[((lambda p, q, u: (p, q, u)), 0)]]
-    direct = chips(mine, far)
     other = cores(mine)
     pieces.append(other)
     plan.append([((lambda p, q, u: (p, 1 - q, u)), 0)])
-    pieces.append(direct)
-    plan.append([((lambda p, q, u: (p ^ far[0], q, u ^ far[1])), 0)])
-    pieces.append(cores(direct))
-    plan.append([((lambda p, q, u: (p ^ far[0], 1 - q, u ^ far[1])), 0)])
     both = jnp.concatenate([mine, other], axis=0)
-    for d0, d1 in rounds:
-        arrived = chips(both, d0, d1)
+    done = {}
+    for number in ORDER:
+        d0, d1, source = STEPS[number]
+        single = source == "own"
+        if source == "own":
+            carried, f0, f1 = mine, (0, 0), (0, 0)
+        elif source == "both":
+            carried, f0, f1 = both, (0, 0), (0, 0)
+        else:
+            carried, f0, f1 = done[source]
+            single = carried.shape[0] == block
+        arrived = chips(carried, d0, d1)
+        d0 = (d0[0] ^ f0[0], d0[1] ^ f0[1])
+        d1 = (d1[0] ^ f1[0], d1[1] ^ f1[1])
+        done[number] = (arrived, d0, d1)
 
         def here(p, q, u, d0=d0, d1=d1):
             return (p ^ jnp.where(q == 0, d0[0], d1[0]), q, u ^ jnp.where(q == 0, d0[1], d1[1]))
@@ -347,9 +355,9 @@
             return z, 1 - s, x
 
         pieces.append(arrived)
-        plan.append([(here, 0), (here_flip, block)])
+        plan.append([(here, 0)] if single else [(here, 0), (here_flip, block)])
         pieces.append(cores(arrived))
-        plan.append([(there, 0), (there_flip, block)])
+        plan.append([(there, 0)] if single else [(there, 0), (there_flip, block)])
     return pieces, plan
 
 

time: 22.3 us -> 19.2 us (0.86)
  waiting for transfers between devices: 8.58 us -> 4.36 us
  starting transfers between devices: 8.51 us -> 9.66 us
    ppermute x4, waiting for transfers between devices: 6.6 us -> 2.72 us  [chips(): return lax.ppermute(value, axes, moves)]
    ppermute x5, starting transfers between devices: 0.54 us -> 2.59 us  [cores(): return lax.ppermute(value, 'section', [(0, 1), (1, 0)])]
    ppermute x4, starting transfers between devices: 7.97 us -> 7.07 us  [chips(): return lax.ppermute(value, axes, moves)]
    ppermute x5, waiting for transfers between devices: 1.99 us -> 1.64 us  [cores(): return lax.ppermute(value, 'section', [(0, 1), (1, 0)])]
  transfers between devices with their start and end apart: 9 -> 9, of which waited for: 6 -> 4; matrix products, arithmetic and copies ran while one was open for 0% -> 0% of each run, Pallas kernels for 0% -> 0%
where the time goes in v2:
time: 19.2 us; the launch traced here: 19.1 us
  starting transfers between devices  9.66 us (50%)
  Pallas kernels  4.87 us (25%)
  waiting for transfers between devices  4.36 us (23%)
    ppermute x4, starting transfers between devices, chips(): return lax.ppermute(value, axes, moves)  7.07 us
    pallas_call x1, Pallas kernels, body(): pl.pallas_call(functools.partial(correlate_kernel, plan, sizes), name='co...  2.75 us
    ppermute x4, waiting for transfers between devices, chips(): return lax.ppermute(value, axes, moves)  2.72 us
    ppermute x5, starting transfers between devices, cores(): return lax.ppermute(value, 'section', [(0, 1), (1, 0)])  2.59 us
    pallas_call x1, Pallas kernels, body(): pl.pallas_call(spectra_kernel, name='spectra', out_shape=pltpu.VMEM((rows...  2.13 us
    ppermute x5, waiting for transfers between devices, cores(): return lax.ppermute(value, 'section', [(0, 1), (1, 0)])  1.64 us
  transfers between devices with their start and end apart: 9, of which 4 were waited for; matrix products, arithmetic and copies ran while one was open for 0% of the time, Pallas kernels for 0%

profile of v2, /device:TPU:0, one launch (start us, length us, event | category | flops | bytes accessed | tf_op | source)
XLA Modules:
  0.0 19.1 jit_solution(15771084389894039133)
XLA Ops:
  0.0 0.0 copy-start.4
  0.0 0.0 copy-start
  0.0 0.0 copy-start.2
  0.0 2.1 %spectra.1.refs_0_ = bf16[128,128]{1,0:T(8,128)(2,1)S(1)} custom-call(s32[2]{0:T(128)} %offsets_hbm.1, f32[1,64]{1,0:T(1,128)} %bitcast.1, bf16[4,24576]{1,0:T(4,128)(2,1)} %raw_hbm.1, bf16[256,256]{1,0:T(8,128)(2,1)} %constant.14.clone.step_a_hbm, f32[32,128]{1,0:T(8,128)} %constant.15.clone.twiddle_hbm, bf16[768,128]{1,0:T(8,128)(2,1)} %constant.16.clone.step_b_hbm, ...), custom_call_target="tpu_custom_call" | custom-call | tf_op jit(solution)/shard_map/spectra/pallas_call | solution.py:378
  2.1 0.0 copy-start.1
  2.2 0.5 %collective-permute-start = (bf16[128,128]{1,0:T(8,128)(2,1)S(1)}, bf16[128,128]{1,0:T(8,128)(2,1)S(1)}, u32[]{:S(2)}, u32[]{:S(2)}) collective-permute-start(bf16[128,128]{1,0:T(8,128)(2,1)S(1)} %spectra.1.refs_0_), channel_id=1, source_target_pairs={{0,2},{2,0},{1,3},{3,1},{4,6},{6,4},{5,7},{7,5},{8,10},{10,8},{9,1... | collective-permute-start | bytes 98312 | tf_op jit(solution)/shard_map/ppermute | solution.py:319
  2.7 0.9 %collective-permute-done.refs_1_ = bf16[128,128]{1,0:T(8,128)(2,1)S(1)} collective-permute-done((bf16[128,128]{1,0:T(8,128)(2,1)S(1)}, bf16[128,128]{1,0:T(8,128)(2,1)S(1)}, u32[]{:S(2)}, u32[]{:S(2)}) %collective-permute-start) | collective-permute-done | bytes 32800 | tf_op jit(solution)/shard_map/ppermute | solution.py:319
  3.5 0.0 copy-start.3
  3.5 4.0 %collective-permute-start.5 = (bf16[256,128]{1,0:T(8,128)(2,1)S(1)}, bf16[256,128]{1,0:T(8,128)(2,1)S(1)}, u32[]{:S(2)}, u32[]{:S(2)}) collective-permute-start(bf16[256,128]{1,0:T(8,128)(2,1)S(1)} %pad_maximum_fusion), channel_id=1, source_target_pairs={{0,8},{2,11},{1,9},{3,10},{4,12},{6,15},{5,13},{7,14},{8,0},{10,3}... | collective-permute-start | bytes 196616 | tf_op jit(solution)/shard_map/ppermute | solution.py:316
  7.5 1.3 %collective-permute-start.3 = (bf16[256,128]{1,0:T(8,128)(2,1)S(1)}, bf16[256,128]{1,0:T(8,128)(2,1)S(1)}, u32[]{:S(2)}, u32[]{:S(2)}) collective-permute-start(bf16[256,128]{1,0:T(8,128)(2,1)S(1)} %pad_maximum_fusion), channel_id=1, source_target_pairs={{0,12},{2,15},{1,13},{3,14},{4,8},{6,11},{5,9},{7,10},{8,4},{10,7}... | collective-permute-start | bytes 196616 | tf_op jit(solution)/shard_map/ppermute | solution.py:316
  8.9 1.5 %collective-permute-start.1 = (bf16[256,128]{1,0:T(8,128)(2,1)S(1)}, bf16[256,128]{1,0:T(8,128)(2,1)S(1)}, u32[]{:S(2)}, u32[]{:S(2)}) collective-permute-start(bf16[256,128]{1,0:T(8,128)(2,1)S(1)} %pad_maximum_fusion), channel_id=1, source_target_pairs={{0,1},{2,7},{1,0},{3,6},{4,5},{6,3},{5,4},{7,2},{8,9},{10,15},{9,8... | collective-permute-start | bytes 196616 | tf_op jit(solution)/shard_map/ppermute | solution.py:316
  10.4 0.2 %collective-permute-start.7 = (bf16[128,128]{1,0:T(8,128)(2,1)S(1)}, bf16[128,128]{1,0:T(8,128)(2,1)S(1)}, u32[]{:S(2)}, u32[]{:S(2)}) collective-permute-start(bf16[128,128]{1,0:T(8,128)(2,1)S(1)} %spectra.1.refs_0_), channel_id=1, source_target_pairs={{0,4},{2,6},{1,5},{3,7},{4,0},{6,2},{5,1},{7,3},{8,12},{10,14},{9,... | collective-permute-start | bytes 98312 | tf_op jit(solution)/shard_map/ppermute | solution.py:316
  10.6 0.0 collective-permute-done.5.refs_6_
  10.6 1.1 %collective-permute-start.6 = (bf16[256,128]{1,0:T(8,128)(2,1)S(1)}, bf16[256,128]{1,0:T(8,128)(2,1)S(1)}, u32[]{:S(2)}, u32[]{:S(2)}) collective-permute-start(bf16[256,128]{1,0:T(8,128)(2,1)S(1)} %collective-permute-done.5.refs_6_), channel_id=1, source_target_pairs={{0,2},{2,0},{1,3},{3,1},{4,6},{6,4},{5,7},{7,5},{8,10},{10,8},{9,1... | collective-permute-start | bytes 196616 | tf_op jit(solution)/shard_map/ppermute | solution.py:319
  11.7 2.5 %collective-permute-done.3.refs_4_ = bf16[256,128]{1,0:T(8,128)(2,1)S(1)} collective-permute-done((bf16[256,128]{1,0:T(8,128)(2,1)S(1)}, bf16[256,128]{1,0:T(8,128)(2,1)S(1)}, u32[]{:S(2)}, u32[]{:S(2)}) %collective-permute-start.3) | collective-permute-done | bytes 65568 | tf_op jit(solution)/shard_map/ppermute | solution.py:316
  14.3 0.5 %collective-permute-start.4 = (bf16[256,128]{1,0:T(8,128)(2,1)S(1)}, bf16[256,128]{1,0:T(8,128)(2,1)S(1)}, u32[]{:S(2)}, u32[]{:S(2)}) collective-permute-start(bf16[256,128]{1,0:T(8,128)(2,1)S(1)} %collective-permute-done.3.refs_4_), channel_id=1, source_target_pairs={{0,2},{2,0},{1,3},{3,1},{4,6},{6,4},{5,7},{7,5},{8,10},{10,8},{9,1... | collective-permute-start | bytes 196616 | tf_op jit(solution)/shard_map/ppermute | solution.py:319
  14.7 0.0 collective-permute-done.1.refs_2_
  14.7 0.1 collective-permute-start.2
  14.8 0.2 collective-permute-done.7.refs_8_
  15.0 0.4 %collective-permute-start.8 = (bf16[128,128]{1,0:T(8,128)(2,1)S(1)}, bf16[128,128]{1,0:T(8,128)(2,1)S(1)}, u32[]{:S(2)}, u32[]{:S(2)}) collective-permute-start(bf16[128,128]{1,0:T(8,128)(2,1)S(1)} %collective-permute-done.7.refs_8_), channel_id=1, source_target_pairs={{0,2},{2,0},{1,3},{3,1},{4,6},{6,4},{5,7},{7,5},{8,10},{10,8},{9,1... | collective-permute-start | bytes 98312 | tf_op jit(solution)/shard_map/ppermute | solution.py:319
  15.4 0.0 copy-done.4
  15.4 0.1 copy.13.table_ref
  15.5 0.8 %collective-permute-done.8.refs_9_ = bf16[128,128]{1,0:T(8,128)(2,1)S(1)} collective-permute-done((bf16[128,128]{1,0:T(8,128)(2,1)S(1)}, bf16[128,128]{1,0:T(8,128)(2,1)S(1)}, u32[]{:S(2)}, u32[]{:S(2)}) %collective-permute-start.8) | collective-permute-done | bytes 32800 | tf_op jit(solution)/shard_map/ppermute | solution.py:319
  16.3 0.0 collective-permute-done.6.refs_7_
  16.3 0.0 collective-permute-done.4.refs_5_
  16.3 0.0 collective-permute-done.2.refs_3_
  16.3 0.0 copy-done
  16.3 0.0 copy-done.2
  16.3 0.0 copy-done.1
  16.3 0.0 copy-done.3
  16.3 2.7 %correlate.1 = f32[2,4,8,2048]{3,2,1,0:T(8,128)} custom-call(s32[32]{0:T(128)S(1)} %copy-done.3, s32[16,2]{1,0:T(8,128)S(1)} %copy.13.table_ref, bf16[256,256]{1,0:T(8,128)(2,1)S(1)} %copy-done.1, f32[32,128]{1,0:T(8,128)S(1)} %copy-done.2, bf16[128,768]{1,0:T(8,128)(2,1)S(1)} %copy-done, bf16[128,128]{1,0:T(8,128)(2,1)S(1)} %spectra.1.refs_0_, ...), custom_call_target="tpu_custom_call" | custom-call | tf_op jit(solution)/shard_map/correlate/pallas_call | solution.py:397
  (1 shorter events, 0.0 us)
Async XLA Ops:
  0.0 15.4 %copy-start.4 = (s32[16,2]{0,1:T(2,128)S(1)}, s32[16,2]{0,1:T(2,128)}, u32[]{:S(2)}) copy-start(s32[16,2]{0,1:T(2,128)} %param.16) | copy-start | bytes 388
  0.0 16.3 %copy-start = (bf16[128,768]{1,0:T(8,128)(2,1)S(1)}, bf16[128,768]{1,0:T(8,128)(2,1)}, u32[]{:S(2)}) copy-start(bf16[128,768]{1,0:T(8,128)(2,1)} %constant.20.clone.step_a_ref) | copy-start | bytes 589828
  0.0 16.3 %copy-start.2 = (f32[32,128]{1,0:T(8,128)S(1)}, f32[32,128]{1,0:T(8,128)}, u32[]{:S(2)}) copy-start(f32[32,128]{1,0:T(8,128)} %constant.19.clone.twiddle_ref) | copy-start | bytes 49156
  2.1 14.2 %copy-start.1 = (bf16[256,256]{1,0:T(8,128)(2,1)S(1)}, bf16[256,256]{1,0:T(8,128)(2,1)}, u32[]{:S(2)}) copy-start(bf16[256,256]{1,0:T(8,128)(2,1)} %constant.18.clone.step_b_ref) | copy-start | bytes 393220
  2.2 1.4 %collective-permute-start = (bf16[128,128]{1,0:T(8,128)(2,1)S(1)}, bf16[128,128]{1,0:T(8,128)(2,1)S(1)}, u32[]{:S(2)}, u32[]{:S(2)}) collective-permute-start(bf16[128,128]{1,0:T(8,128)(2,1)S(1)} %spectra.1.refs_0_), channel_id=1, source_target_pairs={{0,2},{2,0},{1,3},{3,1},{4,6},{6,4},{5,7},{7,5},{8,10},{10,8},{9,1... | collective-permute-start | bytes 98312 | tf_op jit(solution)/shard_map/ppermute | solution.py:319
  3.5 12.8 %copy-start.3 = (s32[32]{0:T(128)S(1)}, s32[32]{0:T(128)}, u32[]{:S(2)}) copy-start(s32[32]{0:T(128)} %ids_ref.1) | copy-start | bytes 388
  3.5 7.1 %collective-permute-start.5 = (bf16[256,128]{1,0:T(8,128)(2,1)S(1)}, bf16[256,128]{1,0:T(8,128)(2,1)S(1)}, u32[]{:S(2)}, u32[]{:S(2)}) collective-permute-start(bf16[256,128]{1,0:T(8,128)(2,1)S(1)} %pad_maximum_fusion), channel_id=1, source_target_pairs={{0,8},{2,11},{1,9},{3,10},{4,12},{6,15},{5,13},{7,14},{8,0},{10,3}... | collective-permute-start | bytes 196616 | tf_op jit(solution)/shard_map/ppermute | solution.py:316
  7.5 6.7 %collective-permute-start.3 = (bf16[256,128]{1,0:T(8,128)(2,1)S(1)}, bf16[256,128]{1,0:T(8,128)(2,1)S(1)}, u32[]{:S(2)}, u32[]{:S(2)}) collective-permute-start(bf16[256,128]{1,0:T(8,128)(2,1)S(1)} %pad_maximum_fusion), channel_id=1, source_target_pairs={{0,12},{2,15},{1,13},{3,14},{4,8},{6,11},{5,9},{7,10},{8,4},{10,7}... | collective-permute-start | bytes 196616 | tf_op jit(solution)/shard_map/ppermute | solution.py:316
  8.9 5.8 %collective-permute-start.1 = (bf16[256,128]{1,0:T(8,128)(2,1)S(1)}, bf16[256,128]{1,0:T(8,128)(2,1)S(1)}, u32[]{:S(2)}, u32[]{:S(2)}) collective-permute-start(bf16[256,128]{1,0:T(8,128)(2,1)S(1)} %pad_maximum_fusion), channel_id=1, source_target_pairs={{0,1},{2,7},{1,0},{3,6},{4,5},{6,3},{5,4},{7,2},{8,9},{10,15},{9,8... | collective-permute-start | bytes 196616 | tf_op jit(solution)/shard_map/ppermute | solution.py:316
  10.4 4.6 %collective-permute-start.7 = (bf16[128,128]{1,0:T(8,128)(2,1)S(1)}, bf16[128,128]{1,0:T(8,128)(2,1)S(1)}, u32[]{:S(2)}, u32[]{:S(2)}) collective-permute-start(bf16[128,128]{1,0:T(8,128)(2,1)S(1)} %spectra.1.refs_0_), channel_id=1, source_target_pairs={{0,4},{2,6},{1,5},{3,7},{4,0},{6,2},{5,1},{7,3},{8,12},{10,14},{9,... | collective-permute-start | bytes 98312 | tf_op jit(solution)/shard_map/ppermute | solution.py:316
  10.6 5.6 %collective-permute-start.6 = (bf16[256,128]{1,0:T(8,128)(2,1)S(1)}, bf16[256,128]{1,0:T(8,128)(2,1)S(1)}, u32[]{:S(2)}, u32[]{:S(2)}) collective-permute-start(bf16[256,128]{1,0:T(8,128)(2,1)S(1)} %collective-permute-done.5.refs_6_), channel_id=1, source_target_pairs={{0,2},{2,0},{1,3},{3,1},{4,6},{6,4},{5,7},{7,5},{8,10},{10,8},{9,1... | collective-permute-start | bytes 196616 | tf_op jit(solution)/shard_map/ppermute | solution.py:319
  14.3 2.0 %collective-permute-start.4 = (bf16[256,128]{1,0:T(8,128)(2,1)S(1)}, bf16[256,128]{1,0:T(8,128)(2,1)S(1)}, u32[]{:S(2)}, u32[]{:S(2)}) collective-permute-start(bf16[256,128]{1,0:T(8,128)(2,1)S(1)} %collective-permute-done.3.refs_4_), channel_id=1, source_target_pairs={{0,2},{2,0},{1,3},{3,1},{4,6},{6,4},{5,7},{7,5},{8,10},{10,8},{9,1... | collective-permute-start | bytes 196616 | tf_op jit(solution)/shard_map/ppermute | solution.py:319
  14.7 1.5 %collective-permute-start.2 = (bf16[256,128]{1,0:T(8,128)(2,1)S(1)}, bf16[256,128]{1,0:T(8,128)(2,1)S(1)}, u32[]{:S(2)}, u32[]{:S(2)}) collective-permute-start(bf16[256,128]{1,0:T(8,128)(2,1)S(1)} %collective-permute-done.1.refs_2_), channel_id=1, source_target_pairs={{0,2},{2,0},{1,3},{3,1},{4,6},{6,4},{5,7},{7,5},{8,10},{10,8},{9,1... | collective-permute-start | bytes 196616 | tf_op jit(solution)/shard_map/ppermute | solution.py:319
  15.0 1.3 %collective-permute-start.8 = (bf16[128,128]{1,0:T(8,128)(2,1)S(1)}, bf16[128,128]{1,0:T(8,128)(2,1)S(1)}, u32[]{:S(2)}, u32[]{:S(2)}) collective-permute-start(bf16[128,128]{1,0:T(8,128)(2,1)S(1)} %collective-permute-done.7.refs_8_), channel_id=1, source_target_pairs={{0,2},{2,0},{1,3},{3,1},{4,6},{6,4},{5,7},{7,5},{8,10},{10,8},{9,1... | collective-permute-start | bytes 98312 | tf_op jit(solution)/shard_map/ppermute | solution.py:319

commit v3 on v2

--- a/solution.py
+++ b/solution.py
@@ -87,40 +87,27 @@
     return high, low
 
 
-def spectra_kernel(
-    offsets_hbm,
-    taps_hbm,
-    raw_hbm,
-    step_a_hbm,
-    twiddle_hbm,
-    step_b_hbm,
-    band_hbm,
-    out_ref,
-    offsets_ref,
-    taps_ref,
-    raw_ref,
-    step_a_ref,
-    twiddle_ref,
-    step_b_ref,
-    band_ref,
-    chunks,
-    padded,
-    arrived,
-):
-    sources = (offsets_hbm, taps_hbm, raw_hbm, step_a_hbm, twiddle_hbm, step_b_hbm, band_hbm)
-    places = (offsets_ref, taps_ref, raw_ref, step_a_ref, twiddle_ref, step_b_ref, band_ref)
+def spectra_kernel(sizes, a_count, *refs):
+    half = (len(refs) - 6) // 2
+    sources, places = refs[:half], refs[half + 2 : 2 * half + 2]
+    out_ref, wanted_ref = refs[half : half + 2]
+    chunks, padded, row_of, arrived = refs[2 * half + 2 :]
+    raw_ref, offsets_ref, taps_ref, ids_ref, table_ref, step_a_ref, twiddle_ref, step_b_ref, band_ref = places
     copies = [
         pltpu.make_async_copy(source, place, arrived.at[q])
         for q, (source, place) in enumerate(zip(sources, places))
     ]
     for copy in copies:
         copy.start()
+    wait_raw, wait_offsets, wait_taps, wait_ids, wait_table, wait_a, wait_t, wait_b, wait_band = [
+        copy.wait for copy in copies
+    ]
     rows = raw_ref.shape[0]
     windows = offsets_ref.shape[0]
     count = rows * windows
     chunk_total = raw_ref.shape[1] // LANES
     padded[...] = jnp.zeros_like(padded)
-    copies[1].wait()
+    wait_taps()
     padded[0:1, 0:TAPS] = taps_ref[...]
     plain = jnp.broadcast_to(padded[0:1, :], padded.shape)
     sublane = lax.broadcasted_iota(jnp.int32, padded.shape, 0)
@@ -129,48 +116,70 @@
         stair = jnp.where(sublane == i, pltpu.roll(plain, DEC * i, 1), stair)
     stair = jnp.concatenate([stair, jnp.zeros((8, 2 * LANES), jnp.float32)], axis=1)
     empty = jnp.zeros((GRAIN, LANES), jnp.float32)
-    parts = []
-    copies[0].wait()
-    copies[2].wait()
+    wait_offsets()
+    starts, filters = [], []
     for w in range(windows):
         start = offsets_ref[w]
         first = jnp.minimum(start // LANES, chunk_total - WINDOW_CHUNKS)
         shift = start - first * LANES
-        slab = raw_ref[:, pl.ds(pl.multiple_of(first * LANES, LANES), WINDOW_CHUNKS * LANES)].astype(
-            jnp.float32
-        )
-        for c in range(WINDOW_CHUNKS):
-            chunks[w, rows * c : rows * (c + 1), :] = slab[:, c * LANES : (c + 1) * LANES]
+        starts.append(pl.multiple_of(first * LANES, LANES))
         band = jnp.concatenate(
             [pltpu.roll(stair, shift + 8 * DEC * g, 1) for g in range(GRAIN // 8)], axis=0
         )
+        columns = []
+        for m in range(6):
+            column = [
+                band[:, (m - g) * LANES : (m - g + 1) * LANES] if 0 <= m - g < 3 else empty
+                for g in range(DEC)
+            ]
+            columns.append(jnp.concatenate(column, axis=0))
+        filters.append(jnp.concatenate(split_terms(jnp.concatenate(columns, axis=1)), axis=0))
+    for wait in (wait_raw, wait_ids, wait_table, wait_a, wait_t, wait_b, wait_band):
+        wait()
+    parts = []
+    for w in range(windows):
+        slab = raw_ref[:, pl.ds(starts[w], WINDOW_CHUNKS * LANES)].astype(jnp.float32)
+        for c in range(WINDOW_CHUNKS):
+            chunks[w, rows * c : rows * (c + 1), :] = slab[:, c * LANES : (c + 1) * LANES]
         left = []
-        filt = []
         for m in range(6):
             pieces = [
                 chunks[w, pl.ds(rows * m + r, COARSE, stride=rows * CHUNK_STEP), :] for r in range(rows)
             ]
             left.append(jnp.concatenate(pieces, axis=0).astype(jnp.bfloat16))
-            column = [
-                band[:, (m - g) * LANES : (m - g + 1) * LANES] if 0 <= m - g < 3 else empty
-                for g in range(DEC)
-            ]
-            filt.append(jnp.concatenate(column, axis=0))
-        left = jnp.concatenate(left, axis=1)
-        filt = jnp.concatenate(split_terms(jnp.concatenate(filt, axis=1)), axis=0)
         both = lax.dot_general(
-            left, filt, (((1,), (1,)), ((), ())), preferred_element_type=jnp.float32
+            jnp.concatenate(left, axis=1),
+            filters[w],
+            (((1,), (1,)), ((), ())),
+            preferred_element_type=jnp.float32,
         )
         parts.append((both[:, :LANES] + both[:, LANES:]).astype(jnp.bfloat16))
     decimated = jnp.concatenate(parts, axis=0)
-    copies[3].wait()
+    pairs, _, subs = sizes
+    channels = ids_ref.shape[0]
+    slots = table_ref.shape[1] // pairs
+    block_rows = a_count * sizes[1] * subs
+    my_pair = lax.axis_index("pairs")
+    first_a = (lax.axis_index("section") * subs + lax.axis_index("sub")) * a_count
+    for c in range(channels):
+        row_of[ids_ref[c]] = c
+    width = 1 + a_count + block_rows
+    for s in range(slots):
+        first_block = table_ref[0, my_pair * slots + s]
+        second_block = table_ref[1, my_pair * slots + s]
+        wanted_ref[s * width] = first_block
+        first_block = jnp.maximum(first_block, 0) * block_rows + first_a
+        second_block = jnp.maximum(second_block, 0) * block_rows
+        for a in range(a_count):
+            wanted_ref[s * width + 1 + a] = row_of[first_block + a]
+        for b in range(block_rows):
+            wanted_ref[s * width + 1 + a_count + b] = row_of[second_block + b]
     coarse = jnp.dot(
         step_a_ref[...], jnp.concatenate([decimated, decimated], axis=0), preferred_element_type=jnp.float32
     )
     size = count * COARSE
     real = coarse[:size].reshape(count, COARSE, LANES)
     imag = coarse[size:].reshape(count, COARSE, LANES)
-    copies[4].wait()
     cos_t = twiddle_ref[:COARSE][None]
     sin_t = twiddle_ref[COARSE:][None]
     turned = jnp.concatenate(
@@ -181,13 +190,11 @@
         axis=1,
     )
     high, low = split_terms(turned)
-    copies[5].wait()
     spectrum = jnp.dot(
         jnp.concatenate([high, low, high], axis=1), step_b_ref[...], preferred_element_type=jnp.float32
     ).reshape(count, COARSE, LANES)
     power = jnp.sum(spectrum * spectrum, axis=1)
     high, low = split_terms(power)
-    copies[6].wait()
     banded = jnp.dot(high, band_ref[...], preferred_element_type=jnp.float32) + jnp.dot(
         low, band_ref[...], preferred_element_type=jnp.float32
     )
@@ -196,23 +203,19 @@
 
 
 def correlate_kernel(
-    plan, groups_of, ids_ref, table_ref, step_b_ref, twiddle_ref, step_a_ref, *refs
+    plan, groups_of, wanted_ref, step_b_ref, twiddle_ref, step_a_ref, *refs
 ):
     piece_refs = refs[: len(plan)]
-    out_ref, gathered, row_of = refs[len(plan) :]
+    out_ref, gathered, staged, sent = refs[len(plan) :]
     pairs, sections, subs = groups_of
-    a_count, slots, block_rows = out_ref.shape[:3]
+    a_count, slots, block_rows = staged.shape[:3]
     rows_total, windows_total = gathered.shape[:2]
-    channels = ids_ref.shape[0]
     rows = rows_total // (pairs * sections)
     windows = windows_total // subs
     tile = rows * windows * COARSE
     my_pair = lax.axis_index("pairs")
     my_section = lax.axis_index("section")
     my_sub = lax.axis_index("sub")
-
-    for c in range(channels):
-        row_of[ids_ref[c]] = c
 
     for ref, blocks in zip(piece_refs, plan):
         for q, (locate, offset) in enumerate(blocks):
@@ -232,24 +235,23 @@
     cos_t = twiddle_ref[:COARSE][None]
     sin_t = twiddle_ref[COARSE:][None]
     size = block_rows * COARSE
-    first_a = (my_section * subs + my_sub) * a_count
+    width = 1 + a_count + block_rows
+
+    def write_out(s):
+        return pltpu.make_async_copy(staged.at[:, s], out_ref.at[:, s], sent.at[s])
 
     def one_slot(s, carry):
-        first_block = table_ref[my_pair * slots + s, 0]
-        second_block = table_ref[my_pair * slots + s, 1]
-        live = jnp.where(first_block >= 0, 1.0, 0.0)
+        live = jnp.where(wanted_ref[s * width] >= 0, 1.0, 0.0)
         scale = weight * live
-        first_block = jnp.maximum(first_block, 0)
-        second_block = jnp.maximum(second_block, 0)
         ones, turns = [], []
         for a in range(a_count):
-            row = row_of[first_block * block_rows + first_a + a]
+            row = wanted_ref[s * width + 1 + a]
             one = [gathered[row, w].astype(jnp.float32) for w in range(windows_total)]
             ones.append(one)
             turns.append([jnp.where(in_left, 1.0, -1.0) * pltpu.roll(v, HALF, 1) for v in one])
         crosses = [[] for _ in range(a_count)]
         for b in range(block_rows):
-            row = row_of[second_block * block_rows + b]
+            row = wanted_ref[s * width + 1 + a_count + b]
             other = [gathered[row, w].astype(jnp.float32) for w in range(windows_total)]
             for a in range(a_count):
                 even = ones[a][0] * other[0]
@@ -273,22 +275,32 @@
             ],
             axis=0,
         )
-        high, low = split_terms(turned)
+        return split_terms(turned)
+
+    def finish(s, turned):
+        high, low = turned
         lags = jnp.dot(
             step_a_ref[...], jnp.concatenate([high, low, high], axis=0), preferred_element_type=jnp.float32
         )
         for a in range(a_count):
             for j2 in range(COARSE):
-                out_ref[a, s, :, j2 * LANES : (j2 + 1) * LANES] = lags[
+                staged[a, s, :, j2 * LANES : (j2 + 1) * LANES] = lags[
                     j2 * block_rows : (j2 + 1) * block_rows, a * LANES : (a + 1) * LANES
                 ]
+        write_out(s).start()
+
+    def whole_slot(s, carry):
+        finish(s, one_slot(s, 0))
         return carry
 
     if slots <= 4:
+        kept = [one_slot(s, 0) for s in range(slots)]
         for s in range(slots):
-            one_slot(s, 0)
+            finish(s, kept[s])
     else:
-        lax.fori_loop(0, slots, one_slot, 0)
+        lax.fori_loop(0, slots, whole_slot, 0)
+    for s in range(slots):
+        write_out(s).wait()
 
 
 def exchange(mine, sizes):
@@ -372,20 +384,28 @@
     vmem = pl.BlockSpec(memory_space=pltpu.VMEM)
     smem = pl.BlockSpec(memory_space=pltpu.SMEM)
 
-    operands = [offsets, fir_taps.reshape(1, TAPS), raw_record]
+    operands = [raw_record, offsets, fir_taps.reshape(1, TAPS), channel_ids, pair_table.T]
     operands += [jnp.asarray(c) for c in forward_constants(rows, windows)]
     operands = [pltpu.with_memory_space_constraint(operand, pltpu.HBM) for operand in operands]
-    whitened = pl.pallas_call(
-        spectra_kernel,
+    in_scalar = (1, 3, 4)
+    wanted_count = slots * (1 + a_count + block_rows)
+    whitened, wanted = pl.pallas_call(
+        functools.partial(spectra_kernel, sizes, a_count),
         name="spectra",
-        out_shape=pltpu.VMEM((rows * windows * COARSE, LANES), jnp.bfloat16),
+        out_shape=(
+            pltpu.VMEM((rows * windows * COARSE, LANES), jnp.bfloat16),
+            pltpu.SMEM((wanted_count,), jnp.int32),
+        ),
         in_specs=[pl.BlockSpec(memory_space=pltpu.HBM)] * len(operands),
-        out_specs=vmem,
-        scratch_shapes=[pltpu.SMEM(offsets.shape, offsets.dtype)]
-        + [pltpu.VMEM(operand.shape, operand.dtype) for operand in operands[1:]]
+        out_specs=(vmem, smem),
+        scratch_shapes=[
+            (pltpu.SMEM if q in in_scalar else pltpu.VMEM)(operand.shape, operand.dtype)
+            for q, operand in enumerate(operands)
+        ]
         + [
             pltpu.VMEM((windows, rows * WINDOW_CHUNKS, LANES), jnp.float32),
             pltpu.VMEM((8, LANES), jnp.float32),
+            pltpu.SMEM(channel_ids.shape, jnp.int32),
             pltpu.SemaphoreType.DMA((len(operands),)),
         ],
         compiler_params=pltpu.CompilerParams(vmem_limit_bytes=32 * 1024 * 1024),
@@ -393,19 +413,22 @@
 
     pieces, plan = exchange(whitened, sizes)
 
+    wanted = pltpu.with_memory_space_constraint(wanted, pltpu.SMEM)
     consts = [jnp.asarray(c) for c in inverse_constants(block_rows)]
+    result = (a_count, slots, block_rows, NF)
     return pl.pallas_call(
         functools.partial(correlate_kernel, plan, sizes),
         name="correlate",
-        out_shape=jax.ShapeDtypeStruct((a_count, slots, block_rows, NF), jnp.float32),
-        in_specs=[smem, smem] + [vmem] * (3 + len(pieces)),
-        out_specs=vmem,
+        out_shape=jax.ShapeDtypeStruct(result, jnp.float32),
+        in_specs=[smem] + [vmem] * (3 + len(pieces)),
+        out_specs=pl.BlockSpec(memory_space=pltpu.HBM),
         scratch_shapes=[
             pltpu.VMEM((rows * pairs * sections, windows * subs, COARSE, LANES), jnp.bfloat16),
-            pltpu.SMEM((channel_ids.shape[0],), jnp.int32),
+            pltpu.VMEM(result, jnp.float32),
+            pltpu.SemaphoreType.DMA((slots,)),
         ],
         compiler_params=pltpu.CompilerParams(vmem_limit_bytes=32 * 1024 * 1024),
-    )(channel_ids, pair_table, *consts, *pieces)
+    )(wanted, *consts, *pieces)
 
 
 def solution(mesh):

time: 19.2 us -> 18.2 us (0.948)
  Pallas kernels: 4.87 us -> 3.89 us
    pallas_call x1, Pallas kernels: 2.75 us -> 1.72 us  [body(): pl.pallas_call(functools.partial(correlate_kernel, plan, sizes), name='co...]
where the time goes in v3:
time: 18.2 us; the launch traced here: 18 us
  starting transfers between devices  9.64 us (53%)
  waiting for transfers between devices  4.42 us (24%)
  Pallas kernels  3.89 us (21%)
    ppermute x4, starting transfers between devices, chips(): return lax.ppermute(value, axes, moves)  7 us
    ppermute x4, waiting for transfers between devices, chips(): return lax.ppermute(value, axes, moves)  2.7 us
    ppermute x5, starting transfers between devices, cores(): return lax.ppermute(value, 'section', [(0, 1), (1, 0)])  2.65 us
    pallas_call x1, Pallas kernels, body(): pl.pallas_call(functools.partial(spectra_kernel, sizes, a_count), name='s...  2.17 us
    ppermute x5, waiting for transfers between devices, cores(): return lax.ppermute(value, 'section', [(0, 1), (1, 0)])  1.72 us
    pallas_call x1, Pallas kernels, body(): pl.pallas_call(functools.partial(correlate_kernel, plan, sizes), name='co...  1.72 us
  transfers between devices with their start and end apart: 9, of which 4 were waited for; matrix products, arithmetic and copies ran while one was open for 0% of the time, Pallas kernels for 0%

profile of v3, /device:TPU:0, one launch (start us, length us, event | category | flops | bytes accessed | tf_op | source)
XLA Modules:
  0.0 18.0 jit_solution(5247193501182181866)
XLA Ops:
  0.0 0.0 copy-start
  0.0 0.0 copy-start.2
  0.0 2.2 %spectra.1 = (bf16[128,128]{1,0:T(8,128)(2,1)S(1)}, s32[44]{0:T(128)S(4)}) custom-call(bf16[4,24576]{1,0:T(4,128)(2,1)} %refs_0_.1, s32[2]{0:T(128)} %refs_1_.1, f32[1,64]{1,0:T(1,128)} %bitcast.3, s32[32]{0:T(128)} %refs_3_.1, s32[2,16]{1,0:T(2,128)} %bitcast.2, bf16[256,256]{1,0:T(8,128)(2,1)} %constant.14.clone.refs_5_, ...), custom_call_target="tpu_custom_call" | custom-call | tf_op jit(solution)/shard_map/spectra/pallas_call | solution.py:392
  2.2 0.0 copy-start.1
  2.2 0.5 %collective-permute-start = (bf16[128,128]{1,0:T(8,128)(2,1)S(1)}, bf16[128,128]{1,0:T(8,128)(2,1)S(1)}, u32[]{:S(2)}, u32[]{:S(2)}) collective-permute-start(bf16[128,128]{1,0:T(8,128)(2,1)S(1)} %get-tuple-element.8.refs_0_), channel_id=1, source_target_pairs={{0,2},{2,0},{1,3},{3,1},{4,6},{6,4},{5,7},{7,5},{8,10},{10,8},{9,1... | collective-permute-start | bytes 98312 | tf_op jit(solution)/shard_map/ppermute | solution.py:331
  2.7 0.9 %collective-permute-done.refs_1_ = bf16[128,128]{1,0:T(8,128)(2,1)S(1)} collective-permute-done((bf16[128,128]{1,0:T(8,128)(2,1)S(1)}, bf16[128,128]{1,0:T(8,128)(2,1)S(1)}, u32[]{:S(2)}, u32[]{:S(2)}) %collective-permute-start) | collective-permute-done | bytes 32800 | tf_op jit(solution)/shard_map/ppermute | solution.py:331
  3.6 3.9 %collective-permute-start.5 = (bf16[256,128]{1,0:T(8,128)(2,1)S(1)}, bf16[256,128]{1,0:T(8,128)(2,1)S(1)}, u32[]{:S(2)}, u32[]{:S(2)}) collective-permute-start(bf16[256,128]{1,0:T(8,128)(2,1)S(1)} %constant_dynamic-update-slice_fusion), channel_id=1, source_target_pairs={{0,8},{2,11},{1,9},{3,10},{4,12},{6,15},{5,13},{7,14},{8,0},{10,3}... | collective-permute-start | bytes 196616 | tf_op jit(solution)/shard_map/ppermute | solution.py:328
  7.5 1.3 %collective-permute-start.3 = (bf16[256,128]{1,0:T(8,128)(2,1)S(1)}, bf16[256,128]{1,0:T(8,128)(2,1)S(1)}, u32[]{:S(2)}, u32[]{:S(2)}) collective-permute-start(bf16[256,128]{1,0:T(8,128)(2,1)S(1)} %constant_dynamic-update-slice_fusion), channel_id=1, source_target_pairs={{0,12},{2,15},{1,13},{3,14},{4,8},{6,11},{5,9},{7,10},{8,4},{10,7}... | collective-permute-start | bytes 196616 | tf_op jit(solution)/shard_map/ppermute | solution.py:328
  8.9 1.5 %collective-permute-start.1 = (bf16[256,128]{1,0:T(8,128)(2,1)S(1)}, bf16[256,128]{1,0:T(8,128)(2,1)S(1)}, u32[]{:S(2)}, u32[]{:S(2)}) collective-permute-start(bf16[256,128]{1,0:T(8,128)(2,1)S(1)} %constant_dynamic-update-slice_fusion), channel_id=1, source_target_pairs={{0,1},{2,7},{1,0},{3,6},{4,5},{6,3},{5,4},{7,2},{8,9},{10,15},{9,8... | collective-permute-start | bytes 196616 | tf_op jit(solution)/shard_map/ppermute | solution.py:328
  10.4 0.2 %collective-permute-start.7 = (bf16[128,128]{1,0:T(8,128)(2,1)S(1)}, bf16[128,128]{1,0:T(8,128)(2,1)S(1)}, u32[]{:S(2)}, u32[]{:S(2)}) collective-permute-start(bf16[128,128]{1,0:T(8,128)(2,1)S(1)} %get-tuple-element.8.refs_0_), channel_id=1, source_target_pairs={{0,4},{2,6},{1,5},{3,7},{4,0},{6,2},{5,1},{7,3},{8,12},{10,14},{9,... | collective-permute-start | bytes 98312 | tf_op jit(solution)/shard_map/ppermute | solution.py:328
  10.6 0.0 collective-permute-done.5.refs_6_
  10.6 1.2 %collective-permute-start.6 = (bf16[256,128]{1,0:T(8,128)(2,1)S(1)}, bf16[256,128]{1,0:T(8,128)(2,1)S(1)}, u32[]{:S(2)}, u32[]{:S(2)}) collective-permute-start(bf16[256,128]{1,0:T(8,128)(2,1)S(1)} %collective-permute-done.5.refs_6_), channel_id=1, source_target_pairs={{0,2},{2,0},{1,3},{3,1},{4,6},{6,4},{5,7},{7,5},{8,10},{10,8},{9,1... | collective-permute-start | bytes 196616 | tf_op jit(solution)/shard_map/ppermute | solution.py:331
  11.8 2.5 %collective-permute-done.3.refs_4_ = bf16[256,128]{1,0:T(8,128)(2,1)S(1)} collective-permute-done((bf16[256,128]{1,0:T(8,128)(2,1)S(1)}, bf16[256,128]{1,0:T(8,128)(2,1)S(1)}, u32[]{:S(2)}, u32[]{:S(2)}) %collective-permute-start.3) | collective-permute-done | bytes 65568 | tf_op jit(solution)/shard_map/ppermute | solution.py:328
  14.3 0.5 %collective-permute-start.4 = (bf16[256,128]{1,0:T(8,128)(2,1)S(1)}, bf16[256,128]{1,0:T(8,128)(2,1)S(1)}, u32[]{:S(2)}, u32[]{:S(2)}) collective-permute-start(bf16[256,128]{1,0:T(8,128)(2,1)S(1)} %collective-permute-done.3.refs_4_), channel_id=1, source_target_pairs={{0,2},{2,0},{1,3},{3,1},{4,6},{6,4},{5,7},{7,5},{8,10},{10,8},{9,1... | collective-permute-start | bytes 196616 | tf_op jit(solution)/shard_map/ppermute | solution.py:331
  14.8 0.0 collective-permute-done.1.refs_2_
  14.8 0.0 collective-permute-start.2
  14.8 0.2 collective-permute-done.7.refs_8_
  15.0 0.4 %collective-permute-start.8 = (bf16[128,128]{1,0:T(8,128)(2,1)S(1)}, bf16[128,128]{1,0:T(8,128)(2,1)S(1)}, u32[]{:S(2)}, u32[]{:S(2)}) collective-permute-start(bf16[128,128]{1,0:T(8,128)(2,1)S(1)} %collective-permute-done.7.refs_8_), channel_id=1, source_target_pairs={{0,2},{2,0},{1,3},{3,1},{4,6},{6,4},{5,7},{7,5},{8,10},{10,8},{9,1... | collective-permute-start | bytes 98312 | tf_op jit(solution)/shard_map/ppermute | solution.py:331
  15.4 0.9 %collective-permute-done.8.refs_9_ = bf16[128,128]{1,0:T(8,128)(2,1)S(1)} collective-permute-done((bf16[128,128]{1,0:T(8,128)(2,1)S(1)}, bf16[128,128]{1,0:T(8,128)(2,1)S(1)}, u32[]{:S(2)}, u32[]{:S(2)}) %collective-permute-start.8) | collective-permute-done | bytes 32800 | tf_op jit(solution)/shard_map/ppermute | solution.py:331
  16.3 0.0 collective-permute-done.6.refs_7_
  16.3 0.0 collective-permute-done.4.refs_5_
  16.3 0.0 collective-permute-done.2.refs_3_
  16.3 0.0 copy-done
  16.3 0.0 copy-done.2
  16.3 0.0 copy-done.1
  16.3 1.7 %correlate.1 = f32[2,4,8,2048]{3,2,1,0:T(8,128)} custom-call(s32[44]{0:T(128)S(4)} %get-tuple-element.7.wanted_ref, bf16[256,256]{1,0:T(8,128)(2,1)S(1)} %copy-done.1, f32[32,128]{1,0:T(8,128)S(1)} %copy-done.2, bf16[128,768]{1,0:T(8,128)(2,1)S(1)} %copy-done, bf16[128,128]{1,0:T(8,128)(2,1)S(1)} %get-tuple-element.8.refs_0_, ...), custom_call_target="tpu_custom_call" | custom-call | tf_op jit(solution)/shard_map/correlate/pallas_call | solution.py:419
  (2 shorter events, 0.0 us)
Async XLA Ops:
  0.0 16.3 %copy-start = (bf16[128,768]{1,0:T(8,128)(2,1)S(1)}, bf16[128,768]{1,0:T(8,128)(2,1)}, u32[]{:S(2)}) copy-start(bf16[128,768]{1,0:T(8,128)(2,1)} %constant.20.clone.step_a_ref) | copy-start | bytes 589828
  0.0 16.3 %copy-start.2 = (f32[32,128]{1,0:T(8,128)S(1)}, f32[32,128]{1,0:T(8,128)}, u32[]{:S(2)}) copy-start(f32[32,128]{1,0:T(8,128)} %constant.19.clone.twiddle_ref) | copy-start | bytes 49156
  2.2 14.1 %copy-start.1 = (bf16[256,256]{1,0:T(8,128)(2,1)S(1)}, bf16[256,256]{1,0:T(8,128)(2,1)}, u32[]{:S(2)}) copy-start(bf16[256,256]{1,0:T(8,128)(2,1)} %constant.18.clone.step_b_ref) | copy-start | bytes 393220
  2.2 1.4 %collective-permute-start = (bf16[128,128]{1,0:T(8,128)(2,1)S(1)}, bf16[128,128]{1,0:T(8,128)(2,1)S(1)}, u32[]{:S(2)}, u32[]{:S(2)}) collective-permute-start(bf16[128,128]{1,0:T(8,128)(2,1)S(1)} %get-tuple-element.8.refs_0_), channel_id=1, source_target_pairs={{0,2},{2,0},{1,3},{3,1},{4,6},{6,4},{5,7},{7,5},{8,10},{10,8},{9,1... | collective-permute-start | bytes 98312 | tf_op jit(solution)/shard_map/ppermute | solution.py:331
  3.6 7.0 %collective-permute-start.5 = (bf16[256,128]{1,0:T(8,128)(2,1)S(1)}, bf16[256,128]{1,0:T(8,128)(2,1)S(1)}, u32[]{:S(2)}, u32[]{:S(2)}) collective-permute-start(bf16[256,128]{1,0:T(8,128)(2,1)S(1)} %constant_dynamic-update-slice_fusion), channel_id=1, source_target_pairs={{0,8},{2,11},{1,9},{3,10},{4,12},{6,15},{5,13},{7,14},{8,0},{10,3}... | collective-permute-start | bytes 196616 | tf_op jit(solution)/shard_map/ppermute | solution.py:328
  7.5 6.8 %collective-permute-start.3 = (bf16[256,128]{1,0:T(8,128)(2,1)S(1)}, bf16[256,128]{1,0:T(8,128)(2,1)S(1)}, u32[]{:S(2)}, u32[]{:S(2)}) collective-permute-start(bf16[256,128]{1,0:T(8,128)(2,1)S(1)} %constant_dynamic-update-slice_fusion), channel_id=1, source_target_pairs={{0,12},{2,15},{1,13},{3,14},{4,8},{6,11},{5,9},{7,10},{8,4},{10,7}... | collective-permute-start | bytes 196616 | tf_op jit(solution)/shard_map/ppermute | solution.py:328
  8.9 5.9 %collective-permute-start.1 = (bf16[256,128]{1,0:T(8,128)(2,1)S(1)}, bf16[256,128]{1,0:T(8,128)(2,1)S(1)}, u32[]{:S(2)}, u32[]{:S(2)}) collective-permute-start(bf16[256,128]{1,0:T(8,128)(2,1)S(1)} %constant_dynamic-update-slice_fusion), channel_id=1, source_target_pairs={{0,1},{2,7},{1,0},{3,6},{4,5},{6,3},{5,4},{7,2},{8,9},{10,15},{9,8... | collective-permute-start | bytes 196616 | tf_op jit(solution)/shard_map/ppermute | solution.py:328
  10.4 4.6 %collective-permute-start.7 = (bf16[128,128]{1,0:T(8,128)(2,1)S(1)}, bf16[128,128]{1,0:T(8,128)(2,1)S(1)}, u32[]{:S(2)}, u32[]{:S(2)}) collective-permute-start(bf16[128,128]{1,0:T(8,128)(2,1)S(1)} %get-tuple-element.8.refs_0_), channel_id=1, source_target_pairs={{0,4},{2,6},{1,5},{3,7},{4,0},{6,2},{5,1},{7,3},{8,12},{10,14},{9,... | collective-permute-start | bytes 98312 | tf_op jit(solution)/shard_map/ppermute | solution.py:328
  10.6 5.7 %collective-permute-start.6 = (bf16[256,128]{1,0:T(8,128)(2,1)S(1)}, bf16[256,128]{1,0:T(8,128)(2,1)S(1)}, u32[]{:S(2)}, u32[]{:S(2)}) collective-permute-start(bf16[256,128]{1,0:T(8,128)(2,1)S(1)} %collective-permute-done.5.refs_6_), channel_id=1, source_target_pairs={{0,2},{2,0},{1,3},{3,1},{4,6},{6,4},{5,7},{7,5},{8,10},{10,8},{9,1... | collective-permute-start | bytes 196616 | tf_op jit(solution)/shard_map/ppermute | solution.py:331
  14.3 2.0 %collective-permute-start.4 = (bf16[256,128]{1,0:T(8,128)(2,1)S(1)}, bf16[256,128]{1,0:T(8,128)(2,1)S(1)}, u32[]{:S(2)}, u32[]{:S(2)}) collective-permute-start(bf16[256,128]{1,0:T(8,128)(2,1)S(1)} %collective-permute-done.3.refs_4_), channel_id=1, source_target_pairs={{0,2},{2,0},{1,3},{3,1},{4,6},{6,4},{5,7},{7,5},{8,10},{10,8},{9,1... | collective-permute-start | bytes 196616 | tf_op jit(solution)/shard_map/ppermute | solution.py:331
  14.8 1.5 %collective-permute-start.2 = (bf16[256,128]{1,0:T(8,128)(2,1)S(1)}, bf16[256,128]{1,0:T(8,128)(2,1)S(1)}, u32[]{:S(2)}, u32[]{:S(2)}) collective-permute-start(bf16[256,128]{1,0:T(8,128)(2,1)S(1)} %collective-permute-done.1.refs_2_), channel_id=1, source_target_pairs={{0,2},{2,0},{1,3},{3,1},{4,6},{6,4},{5,7},{7,5},{8,10},{10,8},{9,1... | collective-permute-start | bytes 196616 | tf_op jit(solution)/shard_map/ppermute | solution.py:331
  15.0 1.3 %collective-permute-start.8 = (bf16[128,128]{1,0:T(8,128)(2,1)S(1)}, bf16[128,128]{1,0:T(8,128)(2,1)S(1)}, u32[]{:S(2)}, u32[]{:S(2)}) collective-permute-start(bf16[128,128]{1,0:T(8,128)(2,1)S(1)} %collective-permute-done.7.refs_8_), channel_id=1, source_target_pairs={{0,2},{2,0},{1,3},{3,1},{4,6},{6,4},{5,7},{7,5},{8,10},{10,8},{9,1... | collective-permute-start | bytes 98312 | tf_op jit(solution)/shard_map/ppermute | solution.py:331

commit v4 on v3

--- a/solution.py
+++ b/solution.py
@@ -20,8 +20,12 @@
 
 CHUNK_STEP = DEC * LANES // LANES
 WINDOW_CHUNKS = CHUNK_STEP * (COARSE - 1) + 6
-STEPS = (((1, 0), (1, 0), 'own'), ((2, 0), (2, 1), 'both'), ((3, 0), (3, 1), 'both'), ((0, 1), (1, 1), 'both'))
-ORDER = (3, 2, 1, 0)
+ROUNDS = (
+    ((0, 1), (1, 1), "both"),
+    ((1, 0), (1, 0), "own"),
+    ((3, 0), (3, 1), "both"),
+    ((2, 0), (2, 1), "both"),
+)
 GRAIN = LANES // DEC
 
 
@@ -275,12 +279,12 @@
             ],
             axis=0,
         )
-        return split_terms(turned)
+        return turned.astype(jnp.bfloat16), None
 
     def finish(s, turned):
         high, low = turned
         lags = jnp.dot(
-            step_a_ref[...], jnp.concatenate([high, low, high], axis=0), preferred_element_type=jnp.float32
+            step_a_ref[:, : 2 * size], high, preferred_element_type=jnp.float32
         )
         for a in range(a_count):
             for j2 in range(COARSE):
@@ -336,21 +340,9 @@
     pieces.append(other)
     plan.append([((lambda p, q, u: (p, 1 - q, u)), 0)])
     both = jnp.concatenate([mine, other], axis=0)
-    done = {}
-    for number in ORDER:
-        d0, d1, source = STEPS[number]
+    for d0, d1, source in ROUNDS:
         single = source == "own"
-        if source == "own":
-            carried, f0, f1 = mine, (0, 0), (0, 0)
-        elif source == "both":
-            carried, f0, f1 = both, (0, 0), (0, 0)
-        else:
-            carried, f0, f1 = done[source]
-            single = carried.shape[0] == block
-        arrived = chips(carried, d0, d1)
-        d0 = (d0[0] ^ f0[0], d0[1] ^ f0[1])
-        d1 = (d1[0] ^ f1[0], d1[1] ^ f1[1])
-        done[number] = (arrived, d0, d1)
+        arrived = chips(mine if single else both, d0, d1)
 
         def here(p, q, u, d0=d0, d1=d1):
             return (p ^ jnp.where(q == 0, d0[0], d1[0]), q, u ^ jnp.where(q == 0, d0[1], d1[1]))

time: 18.2 us -> 18 us (0.989)
  no operation moved by 1% of the time
where the time goes in v4:
time: 18 us; the launch traced here: 17.9 us
  starting transfers between devices  9.64 us (54%)
  waiting for transfers between devices  4.42 us (25%)
  Pallas kernels  3.74 us (21%)
    ppermute x4, starting transfers between devices, chips(): return lax.ppermute(value, axes, moves)  7 us
    ppermute x4, waiting for transfers between devices, chips(): return lax.ppermute(value, axes, moves)  2.7 us
    ppermute x5, starting transfers between devices, cores(): return lax.ppermute(value, 'section', [(0, 1), (1, 0)])  2.65 us
    pallas_call x1, Pallas kernels, body(): pl.pallas_call(functools.partial(spectra_kernel, sizes, a_count), name='s...  2.17 us
    ppermute x5, waiting for transfers between devices, cores(): return lax.ppermute(value, 'section', [(0, 1), (1, 0)])  1.72 us
    pallas_call x1, Pallas kernels, body(): pl.pallas_call(functools.partial(correlate_kernel, plan, sizes), name='co...  1.57 us
  transfers between devices with their start and end apart: 9, of which 4 were waited for; matrix products, arithmetic and copies ran while one was open for 0% of the time, Pallas kernels for 0%

profile of v4, /device:TPU:0, one launch (start us, length us, event | category | flops | bytes accessed | tf_op | source)
XLA Modules:
  0.0 17.9 jit_solution(5673290169574153294)
XLA Ops:
  0.0 0.0 copy-start
  0.0 0.0 copy-start.2
  0.0 2.2 %spectra.1 = (bf16[128,128]{1,0:T(8,128)(2,1)S(1)}, s32[44]{0:T(128)S(4)}) custom-call(bf16[4,24576]{1,0:T(4,128)(2,1)} %refs_0_.1, s32[2]{0:T(128)} %refs_1_.1, f32[1,64]{1,0:T(1,128)} %bitcast.3, s32[32]{0:T(128)} %refs_3_.1, s32[2,16]{1,0:T(2,128)} %bitcast.2, bf16[256,256]{1,0:T(8,128)(2,1)} %constant.14.clone.refs_5_, ...), custom_call_target="tpu_custom_call" | custom-call | tf_op jit(solution)/shard_map/spectra/pallas_call | solution.py:384
  2.2 0.0 copy-start.1
  2.2 0.5 %collective-permute-start = (bf16[128,128]{1,0:T(8,128)(2,1)S(1)}, bf16[128,128]{1,0:T(8,128)(2,1)S(1)}, u32[]{:S(2)}, u32[]{:S(2)}) collective-permute-start(bf16[128,128]{1,0:T(8,128)(2,1)S(1)} %get-tuple-element.8.refs_0_), channel_id=1, source_target_pairs={{0,2},{2,0},{1,3},{3,1},{4,6},{6,4},{5,7},{7,5},{8,10},{10,8},{9,1... | collective-permute-start | bytes 98312 | tf_op jit(solution)/shard_map/ppermute | solution.py:335
  2.7 0.9 %collective-permute-done.refs_1_ = bf16[128,128]{1,0:T(8,128)(2,1)S(1)} collective-permute-done((bf16[128,128]{1,0:T(8,128)(2,1)S(1)}, bf16[128,128]{1,0:T(8,128)(2,1)S(1)}, u32[]{:S(2)}, u32[]{:S(2)}) %collective-permute-start) | collective-permute-done | bytes 32800 | tf_op jit(solution)/shard_map/ppermute | solution.py:335
  3.6 3.9 %collective-permute-start.7 = (bf16[256,128]{1,0:T(8,128)(2,1)S(1)}, bf16[256,128]{1,0:T(8,128)(2,1)S(1)}, u32[]{:S(2)}, u32[]{:S(2)}) collective-permute-start(bf16[256,128]{1,0:T(8,128)(2,1)S(1)} %constant_dynamic-update-slice_fusion), channel_id=1, source_target_pairs={{0,8},{2,11},{1,9},{3,10},{4,12},{6,15},{5,13},{7,14},{8,0},{10,3}... | collective-permute-start | bytes 196616 | tf_op jit(solution)/shard_map/ppermute | solution.py:332
  7.5 1.3 %collective-permute-start.5 = (bf16[256,128]{1,0:T(8,128)(2,1)S(1)}, bf16[256,128]{1,0:T(8,128)(2,1)S(1)}, u32[]{:S(2)}, u32[]{:S(2)}) collective-permute-start(bf16[256,128]{1,0:T(8,128)(2,1)S(1)} %constant_dynamic-update-slice_fusion), channel_id=1, source_target_pairs={{0,12},{2,15},{1,13},{3,14},{4,8},{6,11},{5,9},{7,10},{8,4},{10,7}... | collective-permute-start | bytes 196616 | tf_op jit(solution)/shard_map/ppermute | solution.py:332
  8.9 1.5 %collective-permute-start.1 = (bf16[256,128]{1,0:T(8,128)(2,1)S(1)}, bf16[256,128]{1,0:T(8,128)(2,1)S(1)}, u32[]{:S(2)}, u32[]{:S(2)}) collective-permute-start(bf16[256,128]{1,0:T(8,128)(2,1)S(1)} %constant_dynamic-update-slice_fusion), channel_id=1, source_target_pairs={{0,1},{2,7},{1,0},{3,6},{4,5},{6,3},{5,4},{7,2},{8,9},{10,15},{9,8... | collective-permute-start | bytes 196616 | tf_op jit(solution)/shard_map/ppermute | solution.py:332
  10.4 0.2 %collective-permute-start.3 = (bf16[128,128]{1,0:T(8,128)(2,1)S(1)}, bf16[128,128]{1,0:T(8,128)(2,1)S(1)}, u32[]{:S(2)}, u32[]{:S(2)}) collective-permute-start(bf16[128,128]{1,0:T(8,128)(2,1)S(1)} %get-tuple-element.8.refs_0_), channel_id=1, source_target_pairs={{0,4},{2,6},{1,5},{3,7},{4,0},{6,2},{5,1},{7,3},{8,12},{10,14},{9,... | collective-permute-start | bytes 98312 | tf_op jit(solution)/shard_map/ppermute | solution.py:332
  10.6 0.0 collective-permute-done.7.refs_8_
  10.6 1.2 %collective-permute-start.8 = (bf16[256,128]{1,0:T(8,128)(2,1)S(1)}, bf16[256,128]{1,0:T(8,128)(2,1)S(1)}, u32[]{:S(2)}, u32[]{:S(2)}) collective-permute-start(bf16[256,128]{1,0:T(8,128)(2,1)S(1)} %collective-permute-done.7.refs_8_), channel_id=1, source_target_pairs={{0,2},{2,0},{1,3},{3,1},{4,6},{6,4},{5,7},{7,5},{8,10},{10,8},{9,1... | collective-permute-start | bytes 196616 | tf_op jit(solution)/shard_map/ppermute | solution.py:335
  11.8 2.5 %collective-permute-done.5.refs_6_ = bf16[256,128]{1,0:T(8,128)(2,1)S(1)} collective-permute-done((bf16[256,128]{1,0:T(8,128)(2,1)S(1)}, bf16[256,128]{1,0:T(8,128)(2,1)S(1)}, u32[]{:S(2)}, u32[]{:S(2)}) %collective-permute-start.5) | collective-permute-done | bytes 65568 | tf_op jit(solution)/shard_map/ppermute | solution.py:332
  14.3 0.5 %collective-permute-start.6 = (bf16[256,128]{1,0:T(8,128)(2,1)S(1)}, bf16[256,128]{1,0:T(8,128)(2,1)S(1)}, u32[]{:S(2)}, u32[]{:S(2)}) collective-permute-start(bf16[256,128]{1,0:T(8,128)(2,1)S(1)} %collective-permute-done.5.refs_6_), channel_id=1, source_target_pairs={{0,2},{2,0},{1,3},{3,1},{4,6},{6,4},{5,7},{7,5},{8,10},{10,8},{9,1... | collective-permute-start | bytes 196616 | tf_op jit(solution)/shard_map/ppermute | solution.py:335
  14.8 0.0 collective-permute-done.1.refs_2_
  14.8 0.0 collective-permute-start.2
  14.8 0.2 collective-permute-done.3.refs_4_
  15.0 0.4 %collective-permute-start.4 = (bf16[128,128]{1,0:T(8,128)(2,1)S(1)}, bf16[128,128]{1,0:T(8,128)(2,1)S(1)}, u32[]{:S(2)}, u32[]{:S(2)}) collective-permute-start(bf16[128,128]{1,0:T(8,128)(2,1)S(1)} %collective-permute-done.3.refs_4_), channel_id=1, source_target_pairs={{0,2},{2,0},{1,3},{3,1},{4,6},{6,4},{5,7},{7,5},{8,10},{10,8},{9,1... | collective-permute-start | bytes 98312 | tf_op jit(solution)/shard_map/ppermute | solution.py:335
  15.4 0.9 %collective-permute-done.4.refs_5_ = bf16[128,128]{1,0:T(8,128)(2,1)S(1)} collective-permute-done((bf16[128,128]{1,0:T(8,128)(2,1)S(1)}, bf16[128,128]{1,0:T(8,128)(2,1)S(1)}, u32[]{:S(2)}, u32[]{:S(2)}) %collective-permute-start.4) | collective-permute-done | bytes 32800 | tf_op jit(solution)/shard_map/ppermute | solution.py:335
  16.3 0.0 collective-permute-done.8.refs_9_
  16.3 0.0 collective-permute-done.6.refs_7_
  16.3 0.0 collective-permute-done.2.refs_3_
  16.3 0.0 copy-done
  16.3 0.0 copy-done.2
  16.3 0.0 copy-done.1
  16.3 1.6 %correlate.1 = f32[2,4,8,2048]{3,2,1,0:T(8,128)} custom-call(s32[44]{0:T(128)S(4)} %get-tuple-element.7.wanted_ref, bf16[256,256]{1,0:T(8,128)(2,1)S(1)} %copy-done.1, f32[32,128]{1,0:T(8,128)S(1)} %copy-done.2, bf16[128,768]{1,0:T(8,128)(2,1)S(1)} %copy-done, bf16[128,128]{1,0:T(8,128)(2,1)S(1)} %get-tuple-element.8.refs_0_, ...), custom_call_target="tpu_custom_call" | custom-call | tf_op jit(solution)/shard_map/correlate/pallas_call | solution.py:411
  (2 shorter events, 0.0 us)
Async XLA Ops:
  0.0 16.3 %copy-start = (bf16[128,768]{1,0:T(8,128)(2,1)S(1)}, bf16[128,768]{1,0:T(8,128)(2,1)}, u32[]{:S(2)}) copy-start(bf16[128,768]{1,0:T(8,128)(2,1)} %constant.20.clone.step_a_ref) | copy-start | bytes 589828
  0.0 16.3 %copy-start.2 = (f32[32,128]{1,0:T(8,128)S(1)}, f32[32,128]{1,0:T(8,128)}, u32[]{:S(2)}) copy-start(f32[32,128]{1,0:T(8,128)} %constant.19.clone.twiddle_ref) | copy-start | bytes 49156
  2.2 14.1 %copy-start.1 = (bf16[256,256]{1,0:T(8,128)(2,1)S(1)}, bf16[256,256]{1,0:T(8,128)(2,1)}, u32[]{:S(2)}) copy-start(bf16[256,256]{1,0:T(8,128)(2,1)} %constant.18.clone.step_b_ref) | copy-start | bytes 393220
  2.2 1.4 %collective-permute-start = (bf16[128,128]{1,0:T(8,128)(2,1)S(1)}, bf16[128,128]{1,0:T(8,128)(2,1)S(1)}, u32[]{:S(2)}, u32[]{:S(2)}) collective-permute-start(bf16[128,128]{1,0:T(8,128)(2,1)S(1)} %get-tuple-element.8.refs_0_), channel_id=1, source_target_pairs={{0,2},{2,0},{1,3},{3,1},{4,6},{6,4},{5,7},{7,5},{8,10},{10,8},{9,1... | collective-permute-start | bytes 98312 | tf_op jit(solution)/shard_map/ppermute | solution.py:335
  3.6 7.0 %collective-permute-start.7 = (bf16[256,128]{1,0:T(8,128)(2,1)S(1)}, bf16[256,128]{1,0:T(8,128)(2,1)S(1)}, u32[]{:S(2)}, u32[]{:S(2)}) collective-permute-start(bf16[256,128]{1,0:T(8,128)(2,1)S(1)} %constant_dynamic-update-slice_fusion), channel_id=1, source_target_pairs={{0,8},{2,11},{1,9},{3,10},{4,12},{6,15},{5,13},{7,14},{8,0},{10,3}... | collective-permute-start | bytes 196616 | tf_op jit(solution)/shard_map/ppermute | solution.py:332
  7.5 6.8 %collective-permute-start.5 = (bf16[256,128]{1,0:T(8,128)(2,1)S(1)}, bf16[256,128]{1,0:T(8,128)(2,1)S(1)}, u32[]{:S(2)}, u32[]{:S(2)}) collective-permute-start(bf16[256,128]{1,0:T(8,128)(2,1)S(1)} %constant_dynamic-update-slice_fusion), channel_id=1, source_target_pairs={{0,12},{2,15},{1,13},{3,14},{4,8},{6,11},{5,9},{7,10},{8,4},{10,7}... | collective-permute-start | bytes 196616 | tf_op jit(solution)/shard_map/ppermute | solution.py:332
  8.9 5.9 %collective-permute-start.1 = (bf16[256,128]{1,0:T(8,128)(2,1)S(1)}, bf16[256,128]{1,0:T(8,128)(2,1)S(1)}, u32[]{:S(2)}, u32[]{:S(2)}) collective-permute-start(bf16[256,128]{1,0:T(8,128)(2,1)S(1)} %constant_dynamic-update-slice_fusion), channel_id=1, source_target_pairs={{0,1},{2,7},{1,0},{3,6},{4,5},{6,3},{5,4},{7,2},{8,9},{10,15},{9,8... | collective-permute-start | bytes 196616 | tf_op jit(solution)/shard_map/ppermute | solution.py:332
  10.4 4.6 %collective-permute-start.3 = (bf16[128,128]{1,0:T(8,128)(2,1)S(1)}, bf16[128,128]{1,0:T(8,128)(2,1)S(1)}, u32[]{:S(2)}, u32[]{:S(2)}) collective-permute-start(bf16[128,128]{1,0:T(8,128)(2,1)S(1)} %get-tuple-element.8.refs_0_), channel_id=1, source_target_pairs={{0,4},{2,6},{1,5},{3,7},{4,0},{6,2},{5,1},{7,3},{8,12},{10,14},{9,... | collective-permute-start | bytes 98312 | tf_op jit(solution)/shard_map/ppermute | solution.py:332
  10.6 5.7 %collective-permute-start.8 = (bf16[256,128]{1,0:T(8,128)(2,1)S(1)}, bf16[256,128]{1,0:T(8,128)(2,1)S(1)}, u32[]{:S(2)}, u32[]{:S(2)}) collective-permute-start(bf16[256,128]{1,0:T(8,128)(2,1)S(1)} %collective-permute-done.7.refs_8_), channel_id=1, source_target_pairs={{0,2},{2,0},{1,3},{3,1},{4,6},{6,4},{5,7},{7,5},{8,10},{10,8},{9,1... | collective-permute-start | bytes 196616 | tf_op jit(solution)/shard_map/ppermute | solution.py:335
  14.3 2.0 %collective-permute-start.6 = (bf16[256,128]{1,0:T(8,128)(2,1)S(1)}, bf16[256,128]{1,0:T(8,128)(2,1)S(1)}, u32[]{:S(2)}, u32[]{:S(2)}) collective-permute-start(bf16[256,128]{1,0:T(8,128)(2,1)S(1)} %collective-permute-done.5.refs_6_), channel_id=1, source_target_pairs={{0,2},{2,0},{1,3},{3,1},{4,6},{6,4},{5,7},{7,5},{8,10},{10,8},{9,1... | collective-permute-start | bytes 196616 | tf_op jit(solution)/shard_map/ppermute | solution.py:335
  14.8 1.5 %collective-permute-start.2 = (bf16[256,128]{1,0:T(8,128)(2,1)S(1)}, bf16[256,128]{1,0:T(8,128)(2,1)S(1)}, u32[]{:S(2)}, u32[]{:S(2)}) collective-permute-start(bf16[256,128]{1,0:T(8,128)(2,1)S(1)} %collective-permute-done.1.refs_2_), channel_id=1, source_target_pairs={{0,2},{2,0},{1,3},{3,1},{4,6},{6,4},{5,7},{7,5},{8,10},{10,8},{9,1... | collective-permute-start | bytes 196616 | tf_op jit(solution)/shard_map/ppermute | solution.py:335
  15.0 1.3 %collective-permute-start.4 = (bf16[128,128]{1,0:T(8,128)(2,1)S(1)}, bf16[128,128]{1,0:T(8,128)(2,1)S(1)}, u32[]{:S(2)}, u32[]{:S(2)}) collective-permute-start(bf16[128,128]{1,0:T(8,128)(2,1)S(1)} %collective-permute-done.3.refs_4_), channel_id=1, source_target_pairs={{0,2},{2,0},{1,3},{3,1},{4,6},{6,4},{5,7},{7,5},{8,10},{10,8},{9,1... | collective-permute-start | bytes 98312 | tf_op jit(solution)/shard_map/ppermute | solution.py:335

commit v5 on v4

--- a/solution.py
+++ b/solution.py
@@ -21,10 +21,10 @@
 CHUNK_STEP = DEC * LANES // LANES
 WINDOW_CHUNKS = CHUNK_STEP * (COARSE - 1) + 6
 ROUNDS = (
-    ((0, 1), (1, 1), "both"),
-    ((1, 0), (1, 0), "own"),
-    ((3, 0), (3, 1), "both"),
-    ((2, 0), (2, 1), "both"),
+    ((0, 1), (1, 1)),
+    ((1, 0), (1, 0)),
+    ((3, 0), (3, 1)),
+    ((2, 0), (2, 1)),
 )
 GRAIN = LANES // DEC
 
@@ -340,9 +340,8 @@
     pieces.append(other)
     plan.append([((lambda p, q, u: (p, 1 - q, u)), 0)])
     both = jnp.concatenate([mine, other], axis=0)
-    for d0, d1, source in ROUNDS:
-        single = source == "own"
-        arrived = chips(mine if single else both, d0, d1)
+    for d0, d1 in ROUNDS:
+        arrived = chips(both, d0, d1)
 
         def here(p, q, u, d0=d0, d1=d1):
             return (p ^ jnp.where(q == 0, d0[0], d1[0]), q, u ^ jnp.where(q == 0, d0[1], d1[1]))
@@ -359,9 +358,10 @@
             return z, 1 - s, x
 
         pieces.append(arrived)
-        plan.append([(here, 0)] if single else [(here, 0), (here_flip, block)])
-        pieces.append(cores(arrived))
-        plan.append([(there, 0)] if single else [(there, 0), (there_flip, block)])
+        plan.append([(here, 0), (here_flip, block)])
+        if d0 != d1:
+            pieces.append(cores(arrived))
+            plan.append([(there, 0), (there_flip, block)])
     return pieces, plan
 
 

time: 18 us -> 17.8 us (0.989)
  starting transfers between devices: 9.64 us -> 9.21 us
  waiting for transfers between devices: 4.42 us -> 4.63 us
    ppermute x4, waiting for transfers between devices: 2.7 us -> 3.4 us  [chips(): return lax.ppermute(value, axes, moves)]
    ppermute x5 -> x4, waiting for transfers between devices: 1.72 us -> 1.23 us  [cores(): return lax.ppermute(value, 'section', [(0, 1), (1, 0)])]
    ppermute x5 -> x4, starting transfers between devices: 2.65 us -> 2.22 us  [cores(): return lax.ppermute(value, 'section', [(0, 1), (1, 0)])]
  transfers between devices with their start and end apart: 9 -> 8, of which waited for: 4 -> 4; matrix products, arithmetic and copies ran while one was open for 0% -> 0% of each run, Pallas kernels for 0% -> 0%
where the time goes in v5:
time: 17.8 us; the launch traced here: 17.6 us
  starting transfers between devices  9.21 us (52%)
  waiting for transfers between devices  4.63 us (26%)
  Pallas kernels  3.74 us (21%)
    ppermute x4, starting transfers between devices, chips(): return lax.ppermute(value, axes, moves)  7 us
    ppermute x4, waiting for transfers between devices, chips(): return lax.ppermute(value, axes, moves)  3.4 us
    ppermute x4, starting transfers between devices, cores(): return lax.ppermute(value, 'section', [(0, 1), (1, 0)])  2.22 us
    pallas_call x1, Pallas kernels, body(): pl.pallas_call(functools.partial(spectra_kernel, sizes, a_count), name='s...  2.17 us
    pallas_call x1, Pallas kernels, body(): pl.pallas_call(functools.partial(correlate_kernel, plan, sizes), name='co...  1.57 us
    ppermute x4, waiting for transfers between devices, cores(): return lax.ppermute(value, 'section', [(0, 1), (1, 0)])  1.23 us
  transfers between devices with their start and end apart: 8, of which 4 were waited for; matrix products, arithmetic and copies ran while one was open for 0% of the time, Pallas kernels for 0%

profile of v5, /device:TPU:0, one launch (start us, length us, event | category | flops | bytes accessed | tf_op | source)
XLA Modules:
  0.0 17.6 jit_solution(10766462365806316567)
XLA Ops:
  0.0 0.0 copy-start
  0.0 0.0 copy-start.2
  0.0 2.2 %spectra.1 = (bf16[128,128]{1,0:T(8,128)(2,1)S(1)}, s32[44]{0:T(128)S(4)}) custom-call(bf16[4,24576]{1,0:T(4,128)(2,1)} %refs_0_.1, s32[2]{0:T(128)} %refs_1_.1, f32[1,64]{1,0:T(1,128)} %bitcast.3, s32[32]{0:T(128)} %refs_3_.1, s32[2,16]{1,0:T(2,128)} %bitcast.2, bf16[256,256]{1,0:T(8,128)(2,1)} %constant.14.clone.refs_5_, ...), custom_call_target="tpu_custom_call" | custom-call | tf_op jit(solution)/shard_map/spectra/pallas_call | solution.py:384
  2.2 0.0 copy-start.1
  2.2 0.5 %collective-permute-start = (bf16[128,128]{1,0:T(8,128)(2,1)S(1)}, bf16[128,128]{1,0:T(8,128)(2,1)S(1)}, u32[]{:S(2)}, u32[]{:S(2)}) collective-permute-start(bf16[128,128]{1,0:T(8,128)(2,1)S(1)} %get-tuple-element.8.refs_0_), channel_id=1, source_target_pairs={{0,2},{2,0},{1,3},{3,1},{4,6},{6,4},{5,7},{7,5},{8,10},{10,8},{9,1... | collective-permute-start | bytes 98312 | tf_op jit(solution)/shard_map/ppermute | solution.py:335
  2.7 0.9 %collective-permute-done.refs_1_ = bf16[128,128]{1,0:T(8,128)(2,1)S(1)} collective-permute-done((bf16[128,128]{1,0:T(8,128)(2,1)S(1)}, bf16[128,128]{1,0:T(8,128)(2,1)S(1)}, u32[]{:S(2)}, u32[]{:S(2)}) %collective-permute-start) | collective-permute-done | bytes 32800 | tf_op jit(solution)/shard_map/ppermute | solution.py:335
  3.6 3.9 %collective-permute-start.6 = (bf16[256,128]{1,0:T(8,128)(2,1)S(1)}, bf16[256,128]{1,0:T(8,128)(2,1)S(1)}, u32[]{:S(2)}, u32[]{:S(2)}) collective-permute-start(bf16[256,128]{1,0:T(8,128)(2,1)S(1)} %constant_dynamic-update-slice_fusion), channel_id=1, source_target_pairs={{0,8},{2,11},{1,9},{3,10},{4,12},{6,15},{5,13},{7,14},{8,0},{10,3}... | collective-permute-start | bytes 196616 | tf_op jit(solution)/shard_map/ppermute | solution.py:332
  7.5 1.3 %collective-permute-start.4 = (bf16[256,128]{1,0:T(8,128)(2,1)S(1)}, bf16[256,128]{1,0:T(8,128)(2,1)S(1)}, u32[]{:S(2)}, u32[]{:S(2)}) collective-permute-start(bf16[256,128]{1,0:T(8,128)(2,1)S(1)} %constant_dynamic-update-slice_fusion), channel_id=1, source_target_pairs={{0,12},{2,15},{1,13},{3,14},{4,8},{6,11},{5,9},{7,10},{8,4},{10,7}... | collective-permute-start | bytes 196616 | tf_op jit(solution)/shard_map/ppermute | solution.py:332
  8.9 1.5 %collective-permute-start.1 = (bf16[256,128]{1,0:T(8,128)(2,1)S(1)}, bf16[256,128]{1,0:T(8,128)(2,1)S(1)}, u32[]{:S(2)}, u32[]{:S(2)}) collective-permute-start(bf16[256,128]{1,0:T(8,128)(2,1)S(1)} %constant_dynamic-update-slice_fusion), channel_id=1, source_target_pairs={{0,1},{2,7},{1,0},{3,6},{4,5},{6,3},{5,4},{7,2},{8,9},{10,15},{9,8... | collective-permute-start | bytes 196616 | tf_op jit(solution)/shard_map/ppermute | solution.py:332
  10.4 0.2 %collective-permute-start.3 = (bf16[256,128]{1,0:T(8,128)(2,1)S(1)}, bf16[256,128]{1,0:T(8,128)(2,1)S(1)}, u32[]{:S(2)}, u32[]{:S(2)}) collective-permute-start(bf16[256,128]{1,0:T(8,128)(2,1)S(1)} %constant_dynamic-update-slice_fusion), channel_id=1, source_target_pairs={{0,4},{2,6},{1,5},{3,7},{4,0},{6,2},{5,1},{7,3},{8,12},{10,14},{9,... | collective-permute-start | bytes 196616 | tf_op jit(solution)/shard_map/ppermute | solution.py:332
  10.6 0.0 collective-permute-done.6.refs_7_
  10.6 1.2 %collective-permute-start.7 = (bf16[256,128]{1,0:T(8,128)(2,1)S(1)}, bf16[256,128]{1,0:T(8,128)(2,1)S(1)}, u32[]{:S(2)}, u32[]{:S(2)}) collective-permute-start(bf16[256,128]{1,0:T(8,128)(2,1)S(1)} %collective-permute-done.6.refs_7_), channel_id=1, source_target_pairs={{0,2},{2,0},{1,3},{3,1},{4,6},{6,4},{5,7},{7,5},{8,10},{10,8},{9,1... | collective-permute-start | bytes 196616 | tf_op jit(solution)/shard_map/ppermute | solution.py:335
  11.8 2.5 %collective-permute-done.4.refs_5_ = bf16[256,128]{1,0:T(8,128)(2,1)S(1)} collective-permute-done((bf16[256,128]{1,0:T(8,128)(2,1)S(1)}, bf16[256,128]{1,0:T(8,128)(2,1)S(1)}, u32[]{:S(2)}, u32[]{:S(2)}) %collective-permute-start.4) | collective-permute-done | bytes 65568 | tf_op jit(solution)/shard_map/ppermute | solution.py:332
  14.3 0.5 %collective-permute-start.5 = (bf16[256,128]{1,0:T(8,128)(2,1)S(1)}, bf16[256,128]{1,0:T(8,128)(2,1)S(1)}, u32[]{:S(2)}, u32[]{:S(2)}) collective-permute-start(bf16[256,128]{1,0:T(8,128)(2,1)S(1)} %collective-permute-done.4.refs_5_), channel_id=1, source_target_pairs={{0,2},{2,0},{1,3},{3,1},{4,6},{6,4},{5,7},{7,5},{8,10},{10,8},{9,1... | collective-permute-start | bytes 196616 | tf_op jit(solution)/shard_map/ppermute | solution.py:335
  14.8 0.0 collective-permute-done.1.refs_2_
  14.8 0.0 collective-permute-start.2
  14.8 0.9 %collective-permute-done.3.refs_4_ = bf16[256,128]{1,0:T(8,128)(2,1)S(1)} collective-permute-done((bf16[256,128]{1,0:T(8,128)(2,1)S(1)}, bf16[256,128]{1,0:T(8,128)(2,1)S(1)}, u32[]{:S(2)}, u32[]{:S(2)}) %collective-permute-start.3) | collective-permute-done | bytes 65568 | tf_op jit(solution)/shard_map/ppermute | solution.py:332
  15.7 0.0 collective-permute-done.7.refs_8_
  15.7 0.0 collective-permute-done.5.refs_6_
  15.7 0.4 %collective-permute-done.2.refs_3_ = bf16[256,128]{1,0:T(8,128)(2,1)S(1)} collective-permute-done((bf16[256,128]{1,0:T(8,128)(2,1)S(1)}, bf16[256,128]{1,0:T(8,128)(2,1)S(1)}, u32[]{:S(2)}, u32[]{:S(2)}) %collective-permute-start.2) | collective-permute-done | bytes 65568 | tf_op jit(solution)/shard_map/ppermute | solution.py:335
  16.1 0.0 copy-done
  16.1 0.0 copy-done.2
  16.1 0.0 copy-done.1
  16.1 1.6 %correlate.1 = f32[2,4,8,2048]{3,2,1,0:T(8,128)} custom-call(s32[44]{0:T(128)S(4)} %get-tuple-element.7.wanted_ref, bf16[256,256]{1,0:T(8,128)(2,1)S(1)} %copy-done.1, f32[32,128]{1,0:T(8,128)S(1)} %copy-done.2, bf16[128,768]{1,0:T(8,128)(2,1)S(1)} %copy-done, bf16[128,128]{1,0:T(8,128)(2,1)S(1)} %get-tuple-element.8.refs_0_, ...), custom_call_target="tpu_custom_call" | custom-call | tf_op jit(solution)/shard_map/correlate/pallas_call | solution.py:411
  (2 shorter events, 0.0 us)
Async XLA Ops:
  0.0 16.1 %copy-start = (bf16[128,768]{1,0:T(8,128)(2,1)S(1)}, bf16[128,768]{1,0:T(8,128)(2,1)}, u32[]{:S(2)}) copy-start(bf16[128,768]{1,0:T(8,128)(2,1)} %constant.20.clone.step_a_ref) | copy-start | bytes 589828
  0.0 16.1 %copy-start.2 = (f32[32,128]{1,0:T(8,128)S(1)}, f32[32,128]{1,0:T(8,128)}, u32[]{:S(2)}) copy-start(f32[32,128]{1,0:T(8,128)} %constant.19.clone.twiddle_ref) | copy-start | bytes 49156
  2.2 13.9 %copy-start.1 = (bf16[256,256]{1,0:T(8,128)(2,1)S(1)}, bf16[256,256]{1,0:T(8,128)(2,1)}, u32[]{:S(2)}) copy-start(bf16[256,256]{1,0:T(8,128)(2,1)} %constant.18.clone.step_b_ref) | copy-start | bytes 393220
  2.2 1.4 %collective-permute-start = (bf16[128,128]{1,0:T(8,128)(2,1)S(1)}, bf16[128,128]{1,0:T(8,128)(2,1)S(1)}, u32[]{:S(2)}, u32[]{:S(2)}) collective-permute-start(bf16[128,128]{1,0:T(8,128)(2,1)S(1)} %get-tuple-element.8.refs_0_), channel_id=1, source_target_pairs={{0,2},{2,0},{1,3},{3,1},{4,6},{6,4},{5,7},{7,5},{8,10},{10,8},{9,1... | collective-permute-start | bytes 98312 | tf_op jit(solution)/shard_map/ppermute | solution.py:335
  3.6 7.0 %collective-permute-start.6 = (bf16[256,128]{1,0:T(8,128)(2,1)S(1)}, bf16[256,128]{1,0:T(8,128)(2,1)S(1)}, u32[]{:S(2)}, u32[]{:S(2)}) collective-permute-start(bf16[256,128]{1,0:T(8,128)(2,1)S(1)} %constant_dynamic-update-slice_fusion), channel_id=1, source_target_pairs={{0,8},{2,11},{1,9},{3,10},{4,12},{6,15},{5,13},{7,14},{8,0},{10,3}... | collective-permute-start | bytes 196616 | tf_op jit(solution)/shard_map/ppermute | solution.py:332
  7.5 6.8 %collective-permute-start.4 = (bf16[256,128]{1,0:T(8,128)(2,1)S(1)}, bf16[256,128]{1,0:T(8,128)(2,1)S(1)}, u32[]{:S(2)}, u32[]{:S(2)}) collective-permute-start(bf16[256,128]{1,0:T(8,128)(2,1)S(1)} %constant_dynamic-update-slice_fusion), channel_id=1, source_target_pairs={{0,12},{2,15},{1,13},{3,14},{4,8},{6,11},{5,9},{7,10},{8,4},{10,7}... | collective-permute-start | bytes 196616 | tf_op jit(solution)/shard_map/ppermute | solution.py:332
  8.9 5.9 %collective-permute-start.1 = (bf16[256,128]{1,0:T(8,128)(2,1)S(1)}, bf16[256,128]{1,0:T(8,128)(2,1)S(1)}, u32[]{:S(2)}, u32[]{:S(2)}) collective-permute-start(bf16[256,128]{1,0:T(8,128)(2,1)S(1)} %constant_dynamic-update-slice_fusion), channel_id=1, source_target_pairs={{0,1},{2,7},{1,0},{3,6},{4,5},{6,3},{5,4},{7,2},{8,9},{10,15},{9,8... | collective-permute-start | bytes 196616 | tf_op jit(solution)/shard_map/ppermute | solution.py:332
  10.4 5.3 %collective-permute-start.3 = (bf16[256,128]{1,0:T(8,128)(2,1)S(1)}, bf16[256,128]{1,0:T(8,128)(2,1)S(1)}, u32[]{:S(2)}, u32[]{:S(2)}) collective-permute-start(bf16[256,128]{1,0:T(8,128)(2,1)S(1)} %constant_dynamic-update-slice_fusion), channel_id=1, source_target_pairs={{0,4},{2,6},{1,5},{3,7},{4,0},{6,2},{5,1},{7,3},{8,12},{10,14},{9,... | collective-permute-start | bytes 196616 | tf_op jit(solution)/shard_map/ppermute | solution.py:332
  10.6 5.1 %collective-permute-start.7 = (bf16[256,128]{1,0:T(8,128)(2,1)S(1)}, bf16[256,128]{1,0:T(8,128)(2,1)S(1)}, u32[]{:S(2)}, u32[]{:S(2)}) collective-permute-start(bf16[256,128]{1,0:T(8,128)(2,1)S(1)} %collective-permute-done.6.refs_7_), channel_id=1, source_target_pairs={{0,2},{2,0},{1,3},{3,1},{4,6},{6,4},{5,7},{7,5},{8,10},{10,8},{9,1... | collective-permute-start | bytes 196616 | tf_op jit(solution)/shard_map/ppermute | solution.py:335
  14.3 1.4 %collective-permute-start.5 = (bf16[256,128]{1,0:T(8,128)(2,1)S(1)}, bf16[256,128]{1,0:T(8,128)(2,1)S(1)}, u32[]{:S(2)}, u32[]{:S(2)}) collective-permute-start(bf16[256,128]{1,0:T(8,128)(2,1)S(1)} %collective-permute-done.4.refs_5_), channel_id=1, source_target_pairs={{0,2},{2,0},{1,3},{3,1},{4,6},{6,4},{5,7},{7,5},{8,10},{10,8},{9,1... | collective-permute-start | bytes 196616 | tf_op jit(solution)/shard_map/ppermute | solution.py:335
  14.8 1.3 %collective-permute-start.2 = (bf16[256,128]{1,0:T(8,128)(2,1)S(1)}, bf16[256,128]{1,0:T(8,128)(2,1)S(1)}, u32[]{:S(2)}, u32[]{:S(2)}) collective-permute-start(bf16[256,128]{1,0:T(8,128)(2,1)S(1)} %collective-permute-done.1.refs_2_), channel_id=1, source_target_pairs={{0,2},{2,0},{1,3},{3,1},{4,6},{6,4},{5,7},{7,5},{8,10},{10,8},{9,1... | collective-permute-start | bytes 196616 | tf_op jit(solution)/shard_map/ppermute | solution.py:335

commit v6 on v5

--- a/solution.py
+++ b/solution.py
@@ -68,10 +68,9 @@
     j1 = np.arange(LANES)
     angle_b = 2 * np.pi * np.outer(k2, j1) / LANES
     cos_b, sin_b = np.cos(angle_b), np.sin(angle_b)
-    table = np.concatenate(
-        [np.concatenate([cos_b, sin_b], axis=1), np.concatenate([-sin_b, cos_b], axis=1)], axis=0
-    )
-    step_b = np.concatenate(two_terms(table), axis=0)
+    real_rows = np.concatenate([cos_b, sin_b], axis=1)
+    imag_rows = np.concatenate([-sin_b, cos_b], axis=1)
+    step_b = np.concatenate([real_rows, real_rows, imag_rows, imag_rows], axis=0).astype(ml_dtypes.bfloat16)
     sign = np.where(k1 % 2 == 0, 1.0, -1.0)[:, None] / math.sqrt(NF)
     angle_t = 2 * np.pi * np.outer(k1, j1) / NF
     twiddle = np.concatenate([sign * np.cos(angle_t), sign * np.sin(angle_t)], axis=0)
@@ -263,11 +262,11 @@
                 for w in range(1, windows_total):
                     even = even + ones[a][w] * other[w]
                     odd = odd + turns[a][w] * other[w]
-                cross = jnp.where(in_left, even, odd) + pltpu.roll(jnp.where(in_left, odd, even), HALF, 1)
-                crosses[a].append((cross * scale).astype(jnp.bfloat16))
+                cross = jnp.concatenate([even * scale, odd * scale], axis=1)
+                crosses[a].append(cross.astype(jnp.bfloat16))
         cross = jnp.concatenate([c for per_a in crosses for c in per_a], axis=0)
         fine = jnp.dot(
-            jnp.concatenate([cross, cross], axis=1), step_b_ref[...], preferred_element_type=jnp.float32
+            cross, step_b_ref[...], preferred_element_type=jnp.float32
         ).reshape(a_count * block_rows, COARSE, 2 * LANES)
         real, imag = fine[:, :, :LANES], fine[:, :, LANES:]
         turned_real = (real * cos_t - imag * sin_t).reshape(a_count, size, LANES)

time: 17.8 us -> 17.7 us (level)
  no operation moved by 1% of the time
where the time goes in v6:
time: 17.7 us; the launch traced here: 17.6 us
  starting transfers between devices  9.21 us (52%)
  waiting for transfers between devices  4.63 us (26%)
  Pallas kernels  3.67 us (21%)
    ppermute x4, starting transfers between devices, chips(): return lax.ppermute(value, axes, moves)  7 us
    ppermute x4, waiting for transfers between devices, chips(): return lax.ppermute(value, axes, moves)  3.4 us
    ppermute x4, starting transfers between devices, cores(): return lax.ppermute(value, 'section', [(0, 1), (1, 0)])  2.22 us
    pallas_call x1, Pallas kernels, body(): pl.pallas_call(functools.partial(spectra_kernel, sizes, a_count), name='s...  2.17 us
    pallas_call x1, Pallas kernels, body(): pl.pallas_call(functools.partial(correlate_kernel, plan, sizes), name='co...  1.51 us
    ppermute x4, waiting for transfers between devices, cores(): return lax.ppermute(value, 'section', [(0, 1), (1, 0)])  1.23 us
  transfers between devices with their start and end apart: 8, of which 4 were waited for; matrix products, arithmetic and copies ran while one was open for 0% of the time, Pallas kernels for 0%

profile of v6, /device:TPU:0, one launch (start us, length us, event | category | flops | bytes accessed | tf_op | source)
XLA Modules:
  0.0 17.6 jit_solution(15779972395337480100)
XLA Ops:
  0.0 0.0 copy-start
  0.0 0.0 copy-start.2
  0.0 2.2 %spectra.1 = (bf16[128,128]{1,0:T(8,128)(2,1)S(1)}, s32[44]{0:T(128)S(4)}) custom-call(bf16[4,24576]{1,0:T(4,128)(2,1)} %refs_0_.1, s32[2]{0:T(128)} %refs_1_.1, f32[1,64]{1,0:T(1,128)} %bitcast.3, s32[32]{0:T(128)} %refs_3_.1, s32[2,16]{1,0:T(2,128)} %bitcast.2, bf16[256,256]{1,0:T(8,128)(2,1)} %constant.14.clone.refs_5_, ...), custom_call_target="tpu_custom_call" | custom-call | tf_op jit(solution)/shard_map/spectra/pallas_call | solution.py:383
  2.2 0.0 copy-start.1
  2.2 0.5 %collective-permute-start = (bf16[128,128]{1,0:T(8,128)(2,1)S(1)}, bf16[128,128]{1,0:T(8,128)(2,1)S(1)}, u32[]{:S(2)}, u32[]{:S(2)}) collective-permute-start(bf16[128,128]{1,0:T(8,128)(2,1)S(1)} %get-tuple-element.8.refs_0_), channel_id=1, source_target_pairs={{0,2},{2,0},{1,3},{3,1},{4,6},{6,4},{5,7},{7,5},{8,10},{10,8},{9,1... | collective-permute-start | bytes 98312 | tf_op jit(solution)/shard_map/ppermute | solution.py:334
  2.7 0.9 %collective-permute-done.refs_1_ = bf16[128,128]{1,0:T(8,128)(2,1)S(1)} collective-permute-done((bf16[128,128]{1,0:T(8,128)(2,1)S(1)}, bf16[128,128]{1,0:T(8,128)(2,1)S(1)}, u32[]{:S(2)}, u32[]{:S(2)}) %collective-permute-start) | collective-permute-done | bytes 32800 | tf_op jit(solution)/shard_map/ppermute | solution.py:334
  3.6 3.9 %collective-permute-start.6 = (bf16[256,128]{1,0:T(8,128)(2,1)S(1)}, bf16[256,128]{1,0:T(8,128)(2,1)S(1)}, u32[]{:S(2)}, u32[]{:S(2)}) collective-permute-start(bf16[256,128]{1,0:T(8,128)(2,1)S(1)} %constant_dynamic-update-slice_fusion), channel_id=1, source_target_pairs={{0,8},{2,11},{1,9},{3,10},{4,12},{6,15},{5,13},{7,14},{8,0},{10,3}... | collective-permute-start | bytes 196616 | tf_op jit(solution)/shard_map/ppermute | solution.py:331
  7.5 1.3 %collective-permute-start.4 = (bf16[256,128]{1,0:T(8,128)(2,1)S(1)}, bf16[256,128]{1,0:T(8,128)(2,1)S(1)}, u32[]{:S(2)}, u32[]{:S(2)}) collective-permute-start(bf16[256,128]{1,0:T(8,128)(2,1)S(1)} %constant_dynamic-update-slice_fusion), channel_id=1, source_target_pairs={{0,12},{2,15},{1,13},{3,14},{4,8},{6,11},{5,9},{7,10},{8,4},{10,7}... | collective-permute-start | bytes 196616 | tf_op jit(solution)/shard_map/ppermute | solution.py:331
  8.9 1.5 %collective-permute-start.1 = (bf16[256,128]{1,0:T(8,128)(2,1)S(1)}, bf16[256,128]{1,0:T(8,128)(2,1)S(1)}, u32[]{:S(2)}, u32[]{:S(2)}) collective-permute-start(bf16[256,128]{1,0:T(8,128)(2,1)S(1)} %constant_dynamic-update-slice_fusion), channel_id=1, source_target_pairs={{0,1},{2,7},{1,0},{3,6},{4,5},{6,3},{5,4},{7,2},{8,9},{10,15},{9,8... | collective-permute-start | bytes 196616 | tf_op jit(solution)/shard_map/ppermute | solution.py:331
  10.4 0.2 %collective-permute-start.3 = (bf16[256,128]{1,0:T(8,128)(2,1)S(1)}, bf16[256,128]{1,0:T(8,128)(2,1)S(1)}, u32[]{:S(2)}, u32[]{:S(2)}) collective-permute-start(bf16[256,128]{1,0:T(8,128)(2,1)S(1)} %constant_dynamic-update-slice_fusion), channel_id=1, source_target_pairs={{0,4},{2,6},{1,5},{3,7},{4,0},{6,2},{5,1},{7,3},{8,12},{10,14},{9,... | collective-permute-start | bytes 196616 | tf_op jit(solution)/shard_map/ppermute | solution.py:331
  10.6 0.0 collective-permute-done.6.refs_7_
  10.6 1.2 %collective-permute-start.7 = (bf16[256,128]{1,0:T(8,128)(2,1)S(1)}, bf16[256,128]{1,0:T(8,128)(2,1)S(1)}, u32[]{:S(2)}, u32[]{:S(2)}) collective-permute-start(bf16[256,128]{1,0:T(8,128)(2,1)S(1)} %collective-permute-done.6.refs_7_), channel_id=1, source_target_pairs={{0,2},{2,0},{1,3},{3,1},{4,6},{6,4},{5,7},{7,5},{8,10},{10,8},{9,1... | collective-permute-start | bytes 196616 | tf_op jit(solution)/shard_map/ppermute | solution.py:334
  11.8 2.5 %collective-permute-done.4.refs_5_ = bf16[256,128]{1,0:T(8,128)(2,1)S(1)} collective-permute-done((bf16[256,128]{1,0:T(8,128)(2,1)S(1)}, bf16[256,128]{1,0:T(8,128)(2,1)S(1)}, u32[]{:S(2)}, u32[]{:S(2)}) %collective-permute-start.4) | collective-permute-done | bytes 65568 | tf_op jit(solution)/shard_map/ppermute | solution.py:331
  14.3 0.5 %collective-permute-start.5 = (bf16[256,128]{1,0:T(8,128)(2,1)S(1)}, bf16[256,128]{1,0:T(8,128)(2,1)S(1)}, u32[]{:S(2)}, u32[]{:S(2)}) collective-permute-start(bf16[256,128]{1,0:T(8,128)(2,1)S(1)} %collective-permute-done.4.refs_5_), channel_id=1, source_target_pairs={{0,2},{2,0},{1,3},{3,1},{4,6},{6,4},{5,7},{7,5},{8,10},{10,8},{9,1... | collective-permute-start | bytes 196616 | tf_op jit(solution)/shard_map/ppermute | solution.py:334
  14.8 0.0 collective-permute-done.1.refs_2_
  14.8 0.0 collective-permute-start.2
  14.8 0.9 %collective-permute-done.3.refs_4_ = bf16[256,128]{1,0:T(8,128)(2,1)S(1)} collective-permute-done((bf16[256,128]{1,0:T(8,128)(2,1)S(1)}, bf16[256,128]{1,0:T(8,128)(2,1)S(1)}, u32[]{:S(2)}, u32[]{:S(2)}) %collective-permute-start.3) | collective-permute-done | bytes 65568 | tf_op jit(solution)/shard_map/ppermute | solution.py:331
  15.7 0.0 collective-permute-done.7.refs_8_
  15.7 0.0 collective-permute-done.5.refs_6_
  15.7 0.4 %collective-permute-done.2.refs_3_ = bf16[256,128]{1,0:T(8,128)(2,1)S(1)} collective-permute-done((bf16[256,128]{1,0:T(8,128)(2,1)S(1)}, bf16[256,128]{1,0:T(8,128)(2,1)S(1)}, u32[]{:S(2)}, u32[]{:S(2)}) %collective-permute-start.2) | collective-permute-done | bytes 65568 | tf_op jit(solution)/shard_map/ppermute | solution.py:334
  16.1 0.0 copy-done
  16.1 0.0 copy-done.2
  16.1 0.0 copy-done.1
  16.1 1.5 %correlate.1 = f32[2,4,8,2048]{3,2,1,0:T(8,128)} custom-call(s32[44]{0:T(128)S(4)} %get-tuple-element.7.wanted_ref, bf16[256,256]{1,0:T(8,128)(2,1)S(1)} %copy-done.1, f32[32,128]{1,0:T(8,128)S(1)} %copy-done.2, bf16[128,768]{1,0:T(8,128)(2,1)S(1)} %copy-done, bf16[128,128]{1,0:T(8,128)(2,1)S(1)} %get-tuple-element.8.refs_0_, ...), custom_call_target="tpu_custom_call" | custom-call | tf_op jit(solution)/shard_map/correlate/pallas_call | solution.py:410
  (2 shorter events, 0.0 us)
Async XLA Ops:
  0.0 16.1 %copy-start = (bf16[128,768]{1,0:T(8,128)(2,1)S(1)}, bf16[128,768]{1,0:T(8,128)(2,1)}, u32[]{:S(2)}) copy-start(bf16[128,768]{1,0:T(8,128)(2,1)} %constant.20.clone.step_a_ref) | copy-start | bytes 589828
  0.0 16.1 %copy-start.2 = (f32[32,128]{1,0:T(8,128)S(1)}, f32[32,128]{1,0:T(8,128)}, u32[]{:S(2)}) copy-start(f32[32,128]{1,0:T(8,128)} %constant.19.clone.twiddle_ref) | copy-start | bytes 49156
  2.2 13.9 %copy-start.1 = (bf16[256,256]{1,0:T(8,128)(2,1)S(1)}, bf16[256,256]{1,0:T(8,128)(2,1)}, u32[]{:S(2)}) copy-start(bf16[256,256]{1,0:T(8,128)(2,1)} %constant.18.clone.step_b_ref) | copy-start | bytes 393220
  2.2 1.4 %collective-permute-start = (bf16[128,128]{1,0:T(8,128)(2,1)S(1)}, bf16[128,128]{1,0:T(8,128)(2,1)S(1)}, u32[]{:S(2)}, u32[]{:S(2)}) collective-permute-start(bf16[128,128]{1,0:T(8,128)(2,1)S(1)} %get-tuple-element.8.refs_0_), channel_id=1, source_target_pairs={{0,2},{2,0},{1,3},{3,1},{4,6},{6,4},{5,7},{7,5},{8,10},{10,8},{9,1... | collective-permute-start | bytes 98312 | tf_op jit(solution)/shard_map/ppermute | solution.py:334
  3.6 7.0 %collective-permute-start.6 = (bf16[256,128]{1,0:T(8,128)(2,1)S(1)}, bf16[256,128]{1,0:T(8,128)(2,1)S(1)}, u32[]{:S(2)}, u32[]{:S(2)}) collective-permute-start(bf16[256,128]{1,0:T(8,128)(2,1)S(1)} %constant_dynamic-update-slice_fusion), channel_id=1, source_target_pairs={{0,8},{2,11},{1,9},{3,10},{4,12},{6,15},{5,13},{7,14},{8,0},{10,3}... | collective-permute-start | bytes 196616 | tf_op jit(solution)/shard_map/ppermute | solution.py:331
  7.5 6.8 %collective-permute-start.4 = (bf16[256,128]{1,0:T(8,128)(2,1)S(1)}, bf16[256,128]{1,0:T(8,128)(2,1)S(1)}, u32[]{:S(2)}, u32[]{:S(2)}) collective-permute-start(bf16[256,128]{1,0:T(8,128)(2,1)S(1)} %constant_dynamic-update-slice_fusion), channel_id=1, source_target_pairs={{0,12},{2,15},{1,13},{3,14},{4,8},{6,11},{5,9},{7,10},{8,4},{10,7}... | collective-permute-start | bytes 196616 | tf_op jit(solution)/shard_map/ppermute | solution.py:331
  8.9 5.9 %collective-permute-start.1 = (bf16[256,128]{1,0:T(8,128)(2,1)S(1)}, bf16[256,128]{1,0:T(8,128)(2,1)S(1)}, u32[]{:S(2)}, u32[]{:S(2)}) collective-permute-start(bf16[256,128]{1,0:T(8,128)(2,1)S(1)} %constant_dynamic-update-slice_fusion), channel_id=1, source_target_pairs={{0,1},{2,7},{1,0},{3,6},{4,5},{6,3},{5,4},{7,2},{8,9},{10,15},{9,8... | collective-permute-start | bytes 196616 | tf_op jit(solution)/shard_map/ppermute | solution.py:331
  10.4 5.3 %collective-permute-start.3 = (bf16[256,128]{1,0:T(8,128)(2,1)S(1)}, bf16[256,128]{1,0:T(8,128)(2,1)S(1)}, u32[]{:S(2)}, u32[]{:S(2)}) collective-permute-start(bf16[256,128]{1,0:T(8,128)(2,1)S(1)} %constant_dynamic-update-slice_fusion), channel_id=1, source_target_pairs={{0,4},{2,6},{1,5},{3,7},{4,0},{6,2},{5,1},{7,3},{8,12},{10,14},{9,... | collective-permute-start | bytes 196616 | tf_op jit(solution)/shard_map/ppermute | solution.py:331
  10.6 5.1 %collective-permute-start.7 = (bf16[256,128]{1,0:T(8,128)(2,1)S(1)}, bf16[256,128]{1,0:T(8,128)(2,1)S(1)}, u32[]{:S(2)}, u32[]{:S(2)}) collective-permute-start(bf16[256,128]{1,0:T(8,128)(2,1)S(1)} %collective-permute-done.6.refs_7_), channel_id=1, source_target_pairs={{0,2},{2,0},{1,3},{3,1},{4,6},{6,4},{5,7},{7,5},{8,10},{10,8},{9,1... | collective-permute-start | bytes 196616 | tf_op jit(solution)/shard_map/ppermute | solution.py:334
  14.3 1.4 %collective-permute-start.5 = (bf16[256,128]{1,0:T(8,128)(2,1)S(1)}, bf16[256,128]{1,0:T(8,128)(2,1)S(1)}, u32[]{:S(2)}, u32[]{:S(2)}) collective-permute-start(bf16[256,128]{1,0:T(8,128)(2,1)S(1)} %collective-permute-done.4.refs_5_), channel_id=1, source_target_pairs={{0,2},{2,0},{1,3},{3,1},{4,6},{6,4},{5,7},{7,5},{8,10},{10,8},{9,1... | collective-permute-start | bytes 196616 | tf_op jit(solution)/shard_map/ppermute | solution.py:334
  14.8 1.3 %collective-permute-start.2 = (bf16[256,128]{1,0:T(8,128)(2,1)S(1)}, bf16[256,128]{1,0:T(8,128)(2,1)S(1)}, u32[]{:S(2)}, u32[]{:S(2)}) collective-permute-start(bf16[256,128]{1,0:T(8,128)(2,1)S(1)} %collective-permute-done.1.refs_2_), channel_id=1, source_target_pairs={{0,2},{2,0},{1,3},{3,1},{4,6},{6,4},{5,7},{7,5},{8,10},{10,8},{9,1... | collective-permute-start | bytes 196616 | tf_op jit(solution)/shard_map/ppermute | solution.py:334

commit v7 on v5

--- a/solution.py
+++ b/solution.py
@@ -46,8 +46,7 @@
         for w in range(windows):
             blocks[0, r, w, :, w, r, :] = np.cos(angle_a)
             blocks[1, r, w, :, w, r, :] = -np.sin(angle_a)
-    high, low = two_terms(blocks.reshape(2 * count * COARSE, count * COARSE))
-    step_a = np.concatenate([high, low], axis=1)
+    step_a = blocks.reshape(2 * count * COARSE, count * COARSE).astype(ml_dtypes.bfloat16)
     angle_t = 2 * np.pi * np.outer(k1, fine) / NF
     twiddle = np.concatenate([np.cos(angle_t), -np.sin(angle_t)], axis=0).astype(np.float32)
     angle_b = 2 * np.pi * np.outer(fine, k2) / LANES
@@ -179,7 +178,7 @@
         for b in range(block_rows):
             wanted_ref[s * width + 1 + a_count + b] = row_of[second_block + b]
     coarse = jnp.dot(
-        step_a_ref[...], jnp.concatenate([decimated, decimated], axis=0), preferred_element_type=jnp.float32
+        step_a_ref[...], decimated, preferred_element_type=jnp.float32
     )
     size = count * COARSE
     real = coarse[:size].reshape(count, COARSE, LANES)

time: 17.8 us -> 17.7 us (level)
  no operation moved by 1% of the time
where the time goes in v7:
time: 17.7 us; the launch traced here: 17.6 us
  starting transfers between devices  9.2 us (52%)
  waiting for transfers between devices  4.64 us (26%)
  Pallas kernels  3.67 us (21%)
    ppermute x4, starting transfers between devices, chips(): return lax.ppermute(value, axes, moves)  7 us
    ppermute x4, waiting for transfers between devices, chips(): return lax.ppermute(value, axes, moves)  3.42 us
    ppermute x4, starting transfers between devices, cores(): return lax.ppermute(value, 'section', [(0, 1), (1, 0)])  2.2 us
    pallas_call x1, Pallas kernels, body(): pl.pallas_call(functools.partial(spectra_kernel, sizes, a_count), name='s...  2.1 us
    pallas_call x1, Pallas kernels, body(): pl.pallas_call(functools.partial(correlate_kernel, plan, sizes), name='co...  1.57 us
    ppermute x4, waiting for transfers between devices, cores(): return lax.ppermute(value, 'section', [(0, 1), (1, 0)])  1.22 us
  transfers between devices with their start and end apart: 8, of which 4 were waited for; matrix products, arithmetic and copies ran while one was open for 0% of the time, Pallas kernels for 0%

profile of v7, /device:TPU:0, one launch (start us, length us, event | category | flops | bytes accessed | tf_op | source)
XLA Modules:
  0.0 17.6 jit_solution(2837443306087851578)
XLA Ops:
  0.0 0.0 copy-start
  0.0 0.0 copy-start.2
  0.0 2.1 %spectra.1 = (bf16[128,128]{1,0:T(8,128)(2,1)S(1)}, s32[44]{0:T(128)S(4)}) custom-call(bf16[4,24576]{1,0:T(4,128)(2,1)} %refs_0_.1, s32[2]{0:T(128)} %refs_1_.1, f32[1,64]{1,0:T(1,128)} %bitcast.3, s32[32]{0:T(128)} %refs_3_.1, s32[2,16]{1,0:T(2,128)} %bitcast.2, bf16[256,128]{1,0:T(8,128)(2,1)} %constant.14.clone.refs_5_, ...), custom_call_target="tpu_custom_call" | custom-call | tf_op jit(solution)/shard_map/spectra/pallas_call | solution.py:383
  2.1 0.0 copy-start.1
  2.1 0.5 %collective-permute-start = (bf16[128,128]{1,0:T(8,128)(2,1)S(1)}, bf16[128,128]{1,0:T(8,128)(2,1)S(1)}, u32[]{:S(2)}, u32[]{:S(2)}) collective-permute-start(bf16[128,128]{1,0:T(8,128)(2,1)S(1)} %get-tuple-element.8.refs_0_), channel_id=1, source_target_pairs={{0,2},{2,0},{1,3},{3,1},{4,6},{6,4},{5,7},{7,5},{8,10},{10,8},{9,1... | collective-permute-start | bytes 98312 | tf_op jit(solution)/shard_map/ppermute | solution.py:334
  2.6 0.9 %collective-permute-done.refs_1_ = bf16[128,128]{1,0:T(8,128)(2,1)S(1)} collective-permute-done((bf16[128,128]{1,0:T(8,128)(2,1)S(1)}, bf16[128,128]{1,0:T(8,128)(2,1)S(1)}, u32[]{:S(2)}, u32[]{:S(2)}) %collective-permute-start) | collective-permute-done | bytes 32800 | tf_op jit(solution)/shard_map/ppermute | solution.py:334
  3.5 3.9 %collective-permute-start.6 = (bf16[256,128]{1,0:T(8,128)(2,1)S(1)}, bf16[256,128]{1,0:T(8,128)(2,1)S(1)}, u32[]{:S(2)}, u32[]{:S(2)}) collective-permute-start(bf16[256,128]{1,0:T(8,128)(2,1)S(1)} %constant_dynamic-update-slice_fusion), channel_id=1, source_target_pairs={{0,8},{2,11},{1,9},{3,10},{4,12},{6,15},{5,13},{7,14},{8,0},{10,3}... | collective-permute-start | bytes 196616 | tf_op jit(solution)/shard_map/ppermute | solution.py:331
  7.4 1.3 %collective-permute-start.4 = (bf16[256,128]{1,0:T(8,128)(2,1)S(1)}, bf16[256,128]{1,0:T(8,128)(2,1)S(1)}, u32[]{:S(2)}, u32[]{:S(2)}) collective-permute-start(bf16[256,128]{1,0:T(8,128)(2,1)S(1)} %constant_dynamic-update-slice_fusion), channel_id=1, source_target_pairs={{0,12},{2,15},{1,13},{3,14},{4,8},{6,11},{5,9},{7,10},{8,4},{10,7}... | collective-permute-start | bytes 196616 | tf_op jit(solution)/shard_map/ppermute | solution.py:331
  8.8 1.5 %collective-permute-start.1 = (bf16[256,128]{1,0:T(8,128)(2,1)S(1)}, bf16[256,128]{1,0:T(8,128)(2,1)S(1)}, u32[]{:S(2)}, u32[]{:S(2)}) collective-permute-start(bf16[256,128]{1,0:T(8,128)(2,1)S(1)} %constant_dynamic-update-slice_fusion), channel_id=1, source_target_pairs={{0,1},{2,7},{1,0},{3,6},{4,5},{6,3},{5,4},{7,2},{8,9},{10,15},{9,8... | collective-permute-start | bytes 196616 | tf_op jit(solution)/shard_map/ppermute | solution.py:331
  10.3 0.2 %collective-permute-start.3 = (bf16[256,128]{1,0:T(8,128)(2,1)S(1)}, bf16[256,128]{1,0:T(8,128)(2,1)S(1)}, u32[]{:S(2)}, u32[]{:S(2)}) collective-permute-start(bf16[256,128]{1,0:T(8,128)(2,1)S(1)} %constant_dynamic-update-slice_fusion), channel_id=1, source_target_pairs={{0,4},{2,6},{1,5},{3,7},{4,0},{6,2},{5,1},{7,3},{8,12},{10,14},{9,... | collective-permute-start | bytes 196616 | tf_op jit(solution)/shard_map/ppermute | solution.py:331
  10.5 0.0 collective-permute-done.6.refs_7_
  10.5 1.2 %collective-permute-start.7 = (bf16[256,128]{1,0:T(8,128)(2,1)S(1)}, bf16[256,128]{1,0:T(8,128)(2,1)S(1)}, u32[]{:S(2)}, u32[]{:S(2)}) collective-permute-start(bf16[256,128]{1,0:T(8,128)(2,1)S(1)} %collective-permute-done.6.refs_7_), channel_id=1, source_target_pairs={{0,2},{2,0},{1,3},{3,1},{4,6},{6,4},{5,7},{7,5},{8,10},{10,8},{9,1... | collective-permute-start | bytes 196616 | tf_op jit(solution)/shard_map/ppermute | solution.py:334
  11.7 2.5 %collective-permute-done.4.refs_5_ = bf16[256,128]{1,0:T(8,128)(2,1)S(1)} collective-permute-done((bf16[256,128]{1,0:T(8,128)(2,1)S(1)}, bf16[256,128]{1,0:T(8,128)(2,1)S(1)}, u32[]{:S(2)}, u32[]{:S(2)}) %collective-permute-start.4) | collective-permute-done | bytes 65568 | tf_op jit(solution)/shard_map/ppermute | solution.py:331
  14.2 0.5 %collective-permute-start.5 = (bf16[256,128]{1,0:T(8,128)(2,1)S(1)}, bf16[256,128]{1,0:T(8,128)(2,1)S(1)}, u32[]{:S(2)}, u32[]{:S(2)}) collective-permute-start(bf16[256,128]{1,0:T(8,128)(2,1)S(1)} %collective-permute-done.4.refs_5_), channel_id=1, source_target_pairs={{0,2},{2,0},{1,3},{3,1},{4,6},{6,4},{5,7},{7,5},{8,10},{10,8},{9,1... | collective-permute-start | bytes 196616 | tf_op jit(solution)/shard_map/ppermute | solution.py:334
  14.7 0.0 collective-permute-done.1.refs_2_
  14.7 0.0 collective-permute-start.2
  14.7 0.9 %collective-permute-done.3.refs_4_ = bf16[256,128]{1,0:T(8,128)(2,1)S(1)} collective-permute-done((bf16[256,128]{1,0:T(8,128)(2,1)S(1)}, bf16[256,128]{1,0:T(8,128)(2,1)S(1)}, u32[]{:S(2)}, u32[]{:S(2)}) %collective-permute-start.3) | collective-permute-done | bytes 65568 | tf_op jit(solution)/shard_map/ppermute | solution.py:331
  15.6 0.0 collective-permute-done.7.refs_8_
  15.6 0.0 collective-permute-done.5.refs_6_
  15.6 0.4 %collective-permute-done.2.refs_3_ = bf16[256,128]{1,0:T(8,128)(2,1)S(1)} collective-permute-done((bf16[256,128]{1,0:T(8,128)(2,1)S(1)}, bf16[256,128]{1,0:T(8,128)(2,1)S(1)}, u32[]{:S(2)}, u32[]{:S(2)}) %collective-permute-start.2) | collective-permute-done | bytes 65568 | tf_op jit(solution)/shard_map/ppermute | solution.py:334
  16.0 0.0 copy-done
  16.0 0.0 copy-done.2
  16.0 0.0 copy-done.1
  16.0 1.6 %correlate.1 = f32[2,4,8,2048]{3,2,1,0:T(8,128)} custom-call(s32[44]{0:T(128)S(4)} %get-tuple-element.7.wanted_ref, bf16[256,256]{1,0:T(8,128)(2,1)S(1)} %copy-done.1, f32[32,128]{1,0:T(8,128)S(1)} %copy-done.2, bf16[128,768]{1,0:T(8,128)(2,1)S(1)} %copy-done, bf16[128,128]{1,0:T(8,128)(2,1)S(1)} %get-tuple-element.8.refs_0_, ...), custom_call_target="tpu_custom_call" | custom-call | tf_op jit(solution)/shard_map/correlate/pallas_call | solution.py:410
  (2 shorter events, 0.0 us)
Async XLA Ops:
  0.0 16.0 %copy-start = (bf16[128,768]{1,0:T(8,128)(2,1)S(1)}, bf16[128,768]{1,0:T(8,128)(2,1)}, u32[]{:S(2)}) copy-start(bf16[128,768]{1,0:T(8,128)(2,1)} %constant.20.clone.step_a_ref) | copy-start | bytes 589828
  0.0 16.0 %copy-start.2 = (f32[32,128]{1,0:T(8,128)S(1)}, f32[32,128]{1,0:T(8,128)}, u32[]{:S(2)}) copy-start(f32[32,128]{1,0:T(8,128)} %constant.19.clone.twiddle_ref) | copy-start | bytes 49156
  2.1 13.9 %copy-start.1 = (bf16[256,256]{1,0:T(8,128)(2,1)S(1)}, bf16[256,256]{1,0:T(8,128)(2,1)}, u32[]{:S(2)}) copy-start(bf16[256,256]{1,0:T(8,128)(2,1)} %constant.18.clone.step_b_ref) | copy-start | bytes 393220
  2.1 1.4 %collective-permute-start = (bf16[128,128]{1,0:T(8,128)(2,1)S(1)}, bf16[128,128]{1,0:T(8,128)(2,1)S(1)}, u32[]{:S(2)}, u32[]{:S(2)}) collective-permute-start(bf16[128,128]{1,0:T(8,128)(2,1)S(1)} %get-tuple-element.8.refs_0_), channel_id=1, source_target_pairs={{0,2},{2,0},{1,3},{3,1},{4,6},{6,4},{5,7},{7,5},{8,10},{10,8},{9,1... | collective-permute-start | bytes 98312 | tf_op jit(solution)/shard_map/ppermute | solution.py:334
  3.5 7.0 %collective-permute-start.6 = (bf16[256,128]{1,0:T(8,128)(2,1)S(1)}, bf16[256,128]{1,0:T(8,128)(2,1)S(1)}, u32[]{:S(2)}, u32[]{:S(2)}) collective-permute-start(bf16[256,128]{1,0:T(8,128)(2,1)S(1)} %constant_dynamic-update-slice_fusion), channel_id=1, source_target_pairs={{0,8},{2,11},{1,9},{3,10},{4,12},{6,15},{5,13},{7,14},{8,0},{10,3}... | collective-permute-start | bytes 196616 | tf_op jit(solution)/shard_map/ppermute | solution.py:331
  7.4 6.8 %collective-permute-start.4 = (bf16[256,128]{1,0:T(8,128)(2,1)S(1)}, bf16[256,128]{1,0:T(8,128)(2,1)S(1)}, u32[]{:S(2)}, u32[]{:S(2)}) collective-permute-start(bf16[256,128]{1,0:T(8,128)(2,1)S(1)} %constant_dynamic-update-slice_fusion), channel_id=1, source_target_pairs={{0,12},{2,15},{1,13},{3,14},{4,8},{6,11},{5,9},{7,10},{8,4},{10,7}... | collective-permute-start | bytes 196616 | tf_op jit(solution)/shard_map/ppermute | solution.py:331
  8.8 5.9 %collective-permute-start.1 = (bf16[256,128]{1,0:T(8,128)(2,1)S(1)}, bf16[256,128]{1,0:T(8,128)(2,1)S(1)}, u32[]{:S(2)}, u32[]{:S(2)}) collective-permute-start(bf16[256,128]{1,0:T(8,128)(2,1)S(1)} %constant_dynamic-update-slice_fusion), channel_id=1, source_target_pairs={{0,1},{2,7},{1,0},{3,6},{4,5},{6,3},{5,4},{7,2},{8,9},{10,15},{9,8... | collective-permute-start | bytes 196616 | tf_op jit(solution)/shard_map/ppermute | solution.py:331
  10.3 5.3 %collective-permute-start.3 = (bf16[256,128]{1,0:T(8,128)(2,1)S(1)}, bf16[256,128]{1,0:T(8,128)(2,1)S(1)}, u32[]{:S(2)}, u32[]{:S(2)}) collective-permute-start(bf16[256,128]{1,0:T(8,128)(2,1)S(1)} %constant_dynamic-update-slice_fusion), channel_id=1, source_target_pairs={{0,4},{2,6},{1,5},{3,7},{4,0},{6,2},{5,1},{7,3},{8,12},{10,14},{9,... | collective-permute-start | bytes 196616 | tf_op jit(solution)/shard_map/ppermute | solution.py:331
  10.5 5.1 %collective-permute-start.7 = (bf16[256,128]{1,0:T(8,128)(2,1)S(1)}, bf16[256,128]{1,0:T(8,128)(2,1)S(1)}, u32[]{:S(2)}, u32[]{:S(2)}) collective-permute-start(bf16[256,128]{1,0:T(8,128)(2,1)S(1)} %collective-permute-done.6.refs_7_), channel_id=1, source_target_pairs={{0,2},{2,0},{1,3},{3,1},{4,6},{6,4},{5,7},{7,5},{8,10},{10,8},{9,1... | collective-permute-start | bytes 196616 | tf_op jit(solution)/shard_map/ppermute | solution.py:334
  14.2 1.4 %collective-permute-start.5 = (bf16[256,128]{1,0:T(8,128)(2,1)S(1)}, bf16[256,128]{1,0:T(8,128)(2,1)S(1)}, u32[]{:S(2)}, u32[]{:S(2)}) collective-permute-start(bf16[256,128]{1,0:T(8,128)(2,1)S(1)} %collective-permute-done.4.refs_5_), channel_id=1, source_target_pairs={{0,2},{2,0},{1,3},{3,1},{4,6},{6,4},{5,7},{7,5},{8,10},{10,8},{9,1... | collective-permute-start | bytes 196616 | tf_op jit(solution)/shard_map/ppermute | solution.py:334
  14.7 1.3 %collective-permute-start.2 = (bf16[256,128]{1,0:T(8,128)(2,1)S(1)}, bf16[256,128]{1,0:T(8,128)(2,1)S(1)}, u32[]{:S(2)}, u32[]{:S(2)}) collective-permute-start(bf16[256,128]{1,0:T(8,128)(2,1)S(1)} %collective-permute-done.1.refs_2_), channel_id=1, source_target_pairs={{0,2},{2,0},{1,3},{3,1},{4,6},{6,4},{5,7},{7,5},{8,10},{10,8},{9,1... | collective-permute-start | bytes 196616 | tf_op jit(solution)/shard_map/ppermute | solution.py:334
